TPU v7x, 128 devices: a whole 4x4x4 slice. The times are simulated.
128 devices in a mesh: row: 4 (over x_hi, core), col: 8 (over y, x_lo), day: 4 (over z).
Axes of the slice: x: 4 (x_hi: 2, x_lo: 2; x = x_hi * 2 + x_lo), y: 4, z: 4, core: 2. Of those that a mesh axis runs over, the one named last changes fastest.
Arguments:
- spectra: bfloat16 [64, 2, 512, 256], P('day', None, ('col', 'row')), may hold values from -12 to 12
- validity: int32 [64, 512], P('day', ('col', 'row')), may hold values from 0 to 1, as said below
Outputs:
- correlations: float32 [512, 512, 512], P('row', 'col', 'day')
Inputs may be any that keep to these rules, and one draw needn't show every extreme that they name: `validity`: 1 marks a usable window of a channel; each channel has its own share of usable windows, and some channels have none.
All inputs are finite; a program needn't handle non-finite values.
Results may differ from a plain program's by a relative error of at most 0.0003.
Values may be sent and summed in bfloat16 or wider, within the bound.
A program may use at most 128 MiB of HBM per device.

v0:
```python
import math

import jax
import jax.numpy as jnp
from jax import lax
from jax.sharding import PartitionSpec as P

F = 256
LAGS = 512


def lag_table(lag_total, freq_total):
    lag_index = lax.iota(jnp.int32, lag_total) - lag_total // 2
    freq_index = lax.iota(jnp.int32, freq_total)
    product_mod = jnp.mod(lag_index[:, None] * freq_index[None, :], 2 * freq_total)
    phases = 2.0 * math.pi / (2 * freq_total) * product_mod.astype(jnp.float32)
    return jnp.stack([jnp.cos(phases), -jnp.sin(phases)]) / math.sqrt(freq_total)


def pair_spectra(row_side, col_side):
    swapped = jnp.stack([row_side[:, 1], -row_side[:, 0]], axis=1)
    left_side = jnp.stack([row_side, swapped])
    return jnp.einsum("swcif,wcjf->sijf", left_side, col_side, preferred_element_type=jnp.float32)


def local_counts(row_flag, col_flag):
    row_valid = row_flag[:, 0, :, 0]
    col_valid = col_flag[:, 0, :, 0]
    return jnp.dot(row_valid.T, col_valid, preferred_element_type=jnp.float32)


def per_device(spectra, validity):
    rows_count = lax.axis_size("row")
    cols_count = lax.axis_size("col")
    row_at = lax.axis_index("row")
    valid_flags = validity.astype(jnp.bfloat16)[:, None, :, None]
    col_spec, col_flag = (
        lax.all_gather(spectra, "row", axis=2, tiled=True),
        lax.all_gather(valid_flags, "row", axis=2, tiled=True),
    )
    width_col = col_spec.shape[2]
    width_row = width_col * cols_count // rows_count
    all_spec, all_flag = (
        lax.all_gather(col_spec, "col", axis=2, tiled=True),
        lax.all_gather(col_flag, "col", axis=2, tiled=True),
    )
    row_start = row_at * width_row
    row_spec = lax.dynamic_slice_in_dim(all_spec, row_start, width_row, 2)
    row_flag = lax.dynamic_slice_in_dim(all_flag, row_start, width_row, 2)
    table = lag_table(LAGS, F)
    stacked = pair_spectra(row_spec * row_flag, col_spec * col_flag)
    numerator = lax.psum_scatter(
        jnp.einsum("stf,sijf->tij", table, stacked, precision=lax.Precision.HIGHEST),
        "day",
        scatter_dimension=0,
        tiled=True,
    )
    pair_total = lax.psum(local_counts(row_flag, col_flag).astype(jnp.bfloat16), "day").astype(
        jnp.float32
    )
    return jnp.transpose(numerator, (1, 2, 0)) / jnp.maximum(pair_total, 1.0)[:, :, None]


def solution(mesh):
    placed = (P("day", None, ("col", "row"), None), P("day", ("col", "row")))
    return jax.shard_map(
        per_device, mesh=mesh, in_specs=placed, out_specs=P("row", "col", "day"), check_vma=False
    )
```

profile of v0, /device:TPU:16, one launch (start us, length us, event | category | flops | bytes accessed | tf_op | source)
XLA Modules:
  0.0 425.7 jit_solution(13945689421851983254)
XLA Ops:
  6.5 1.8 copy.14
  8.4 23.6 %all-gather.6.cloned.1.call-done = bf16[16,2,64,256]{3,0,1,2:T(8,128)(2,1)} async-done(((bf16[16,2,16,256]{3,0,1,2:T(8,128)(2,1)}), bf16[16,2,64,256]{3,0,1,2:T(8,128)(2,1)}) %all-gather.6.cloned.1.call-update) | async-done | bytes 1048592 | tf_op jit(solution)/shard_map/all_gather | solution.py:38
  32.1 0.8 copy.15
  32.9 6.7 %all-gather = bf16[16,64]{0,1:T(8,128)(2,1)S(1)} all-gather(bf16[16,16]{0,1:T(8,128)(2,1)S(1)} %convert_element_type.26), channel_id=2, replica_groups=mesh['row'=4,'col'=8,'day'=4] {'row'}, dimensions={1}, use_global_device_ids=true | all-gather | bytes 2560 | tf_op jit(solution)/shard_map/all_gather | solution.py:39
  39.7 24.6 %all-gather.2 = bf16[8,64,16]{1,2,0:T(8,128)(2,1)S(1)} all-gather(bf16[1,64,16]{1,2,0:T(8,128)(2,1)S(1)} %copy.17), channel_id=3, replica_groups=mesh['row'=4,'col'=8,'day'=4] {'col'}, dimensions={0}, use_global_device_ids=true | all-gather | bytes 18432 | tf_op jit(solution)/shard_map/all_gather | solution.py:45
  64.2 0.1 reshape.111
  64.4 2.1 fusion.19
  66.5 0.2 multiply_bitcast_fusion
  66.7 4.4 %copy.23 = bf16[16,2,64,256,1]{2,0,1,4,3:T(8,128)(2,1)} copy(bf16[16,2,64,256,1]{3,0,1,2,4:T(8,128)(2,1)S(1)} %multiply_bitcast_fusion) | data formatting | bytes 2097152 | tf_op jit(solution)/shard_map/mul | solution.py:51
  71.1 130.9 %all-gather.8.cloned.1.call-done = bf16[16,2,512,256]{3,0,1,2:T(8,128)(2,1)} async-done(((bf16[16,2,64,256]{3,0,1,2:T(8,128)(2,1)}), bf16[16,2,512,256]{3,0,1,2:T(8,128)(2,1)}) %all-gather.8.cloned.1.call-update) | async-done | bytes 8388624 | tf_op jit(solution)/shard_map/all_gather | solution.py:44
  202.1 3.1 constant_dynamic-slice_fusion
  205.2 4.3 %copy.28 = bf16[16,2,128,256]{2,0,1,3:T(8,128)(2,1)S(1)} copy(bf16[16,2,128,256]{3,0,1,2:T(8,128)(2,1)} %constant_dynamic-slice_fusion) | data formatting | bytes 4194304
  209.5 0.1 fusion.28
  209.7 0.1 broadcast_multiply_fusion
  209.8 0.2 fusion.25
  210.0 1.5 maximum_bitcast_fusion
  211.6 0.8 copy-done
  212.4 4.0 convolution_bitcast_fusion
  216.3 43.1 %fusion.2 = f32[512,128,64]{1,0,2:T(8,128)} fusion(f32[2,128,64,256]{1,2,0,3:T(8,128)S(1)} %convolution_bitcast_fusion, f32[1,512,256]{2,1,0:T(8,128)S(1)} %get-tuple-element.8, f32[1,512,256]{2,1,0:T(8,128)S(1)} %get-tuple-element.7), kind=kOutput, calls=%fused_computation.3 | convolution fusion | flops 25770328064 | bytes 34603008 | tf_op jit(solution)/shard_map/stf,sijf->tij/dot_general | solution.py:53
  259.5 0.1 convolution_convert_fusion
  259.6 17.2 %psum.7 = bf16[128,64]{0,1:T(8,128)(2,1)S(1)} all-reduce(bf16[128,64]{0,1:T(8,128)(2,1)S(1)} %convolution_convert_fusion), channel_id=1, replica_groups=mesh['row'=4,'col'=8,'day'=4] {'day'}, use_global_device_ids=true, to_apply=%region_1.2 | all-reduce | flops 8192 | bytes 32768 | tf_op jit(solution)/shard_map/psum | solution.py:58
  276.9 131.9 %reduce-scatter.2.cloned.1.call-done = f32[128,128,64]{1,0,2:T(8,128)} async-done(((f32[512,128,64]{1,0,2:T(8,128)}), f32[128,128,64]{1,0,2:T(8,128)}) %reduce-scatter.2.cloned.1.call-update) | async-done | bytes 4194320 | tf_op jit(solution)/shard_map/reduce_scatter | solution.py:52
  408.8 5.1 %divide_bitcast_fusion = f32[128,64,128]{0,2,1:T(8,128)} fusion(f32[128,128,64]{1,0,2:T(8,128)} %reduce-scatter.2.cloned.1.call-done, f32[128,64]{0,1:T(8,128)S(1)} %convert_maximum_fusion), kind=kLoop, calls=%fused_computation.7 | loop fusion | flops 1048576 | bytes 8421376 | tf_op jit(solution)/shard_map/div | solution.py:61
  413.9 5.3 %copy.22 = f32[128,64,128]{2,1,0:T(8,128)} copy(f32[128,64,128]{0,2,1:T(8,128)} %divide_bitcast_fusion) | data formatting | bytes 8388608 | tf_op jit(solution)/shard_map/div | solution.py:61
  (15 shorter events, 0.3 us)
Async XLA Ops:
  6.5 25.5 %all-gather.6.cloned.1.call-start = ((), (), s32[]{:S(2)}) async-start(), calls=%async_computation.1 | async-start | bytes 1310720 | tf_op jit(solution)/shard_map/all_gather | solution.py:38
  8.4 193.7 %all-gather.8.cloned.1.call-start = ((), (), s32[]{:S(2)}) async-start(), calls=%async_computation.2 | async-start | bytes 9437184 | tf_op jit(solution)/shard_map/all_gather | solution.py:44
  32.0 34.5 %copy-start.1 = (bf16[16,2,64,256]{3,0,1,2:T(8,128)(2,1)S(1)}, bf16[16,2,64,256]{3,0,1,2:T(8,128)(2,1)}, u32[]{:S(2)}) copy-start(bf16[16,2,64,256]{3,0,1,2:T(8,128)(2,1)} %all-gather.6.cloned.1.call-done) | copy-start | bytes 3145732
  32.0 376.8 %reduce-scatter.2.cloned.1.call-start = ((), (), s32[]{:S(2)}) async-start(), calls=%async_computation.3 | async-start | bytes 20971520 | tf_op jit(solution)/shard_map/reduce_scatter | solution.py:52
  210.0 2.4 copy-start
Sparse Core Ops, SparseCore 0:
  9.0 22.9 all-gather.5
  33.6 168.3 all-gather.7
  259.6 149.1 reduce-scatter.1
where the time goes:
time: 427 us; the launch traced here: 426 us
  waiting for transfers between devices  287 us (67%)
  blocking collectives  48.4 us (11%)
  matrix products  47.3 us (11%)
  local copies, waits for them, and re-layouts  20.8 us (5%)
  between operations  13.2 us (3%)
  other arithmetic  9.43 us (2%)
    reduce_scatter x1, waiting for transfers between devices, per_device(): lax.psum_scatter(jnp.einsum('stf,sijf->tij', table, stacked, precision=la...  132 us
    all_gather x1, waiting for transfers between devices, per_device(): lax.all_gather(col_spec, 'col', axis=2, tiled=True)  131 us
    dot_general x1, matrix products, per_device(): jnp.einsum('stf,sijf->tij', table, stacked, precision=lax.Precision.HIGHEST)  43.1 us
    all_gather x1, blocking collectives, per_device(): lax.all_gather(col_flag, 'col', axis=2, tiled=True)  24.6 us
    all_gather x1, waiting for transfers between devices, per_device(): lax.all_gather(spectra, 'row', axis=2, tiled=True)  23.6 us
    psum x1, blocking collectives, per_device(): lax.psum(local_counts(row_flag, col_flag).astype(jnp.bfloat16), 'day')  17.2 us
  transfers between devices with their start and end apart: 3, of which 3 were waited for; matrix products, arithmetic and copies ran while one was open for 2% of the time, Pallas kernels for 0%

commit v1 on v0

v1 whole, which is shorter than its diff:
```python
import math

import jax
import jax.numpy as jnp
import ml_dtypes
import numpy as np
from jax import lax
from jax.experimental import pallas as pl
from jax.experimental.pallas import tpu as pltpu
from jax.sharding import PartitionSpec as P

F = 256
LAGS = 512
ROWS, COLS, DAYS = 4, 8, 4
PACK = 4
GROUPS = F // PACK
SLOTS = GROUPS + 1
WIDE = 128
CHUNKS = [(0, 9)] + [(1 + 8 * k, 8) for k in range(1, 8)]
ORDER = (0, 2, 1, 3)
MESH = pl.DeviceIdType.MESH
NT = (((1,), (1,)), ((), ()))


def lag_tables():
    lag = np.arange(LAGS) - LAGS // 2
    freq = np.arange(F)
    phase = 2.0 * math.pi / (2 * F) * np.mod(lag[:, None] * freq[None, :], 2 * F)
    both = np.stack([np.cos(phase), -np.sin(phase)]) / math.sqrt(F)
    both = both.reshape(2, DAYS, LAGS // DAYS, PACK, GROUPS).transpose(1, 2, 4, 3, 0)
    both = both.reshape(DAYS, LAGS // DAYS, 2 * F).astype(np.float32)
    high = both.astype(ml_dtypes.bfloat16)
    low = (both - high.astype(np.float32)).astype(ml_dtypes.bfloat16)
    return np.concatenate([high, low], axis=1)


def own_unit(spectra, validity):
    windows, _, channels, _ = spectra.shape
    flags = validity.astype(jnp.bfloat16)
    cleaned = spectra * flags[:, None, :, None]
    split = cleaned.reshape(windows, 2, channels, PACK, GROUPS)
    packed = jnp.transpose(split, (4, 2, 3, 1, 0)).reshape(GROUPS, channels, WIDE)
    first = jnp.pad(flags.T, ((0, 0), (0, WIDE - windows)))
    return jnp.concatenate([first[None], packed])


def gather_kernel(unit, near, full, recv, sent, here):
    row, col, day = lax.axis_index("row"), lax.axis_index("col"), lax.axis_index("day")
    core, x_lo, y = row % 2, col % 2, col // 2
    sibling = {"row": row + 1 - 2 * core}
    opposite = {"row": (row + 2) % ROWS}
    partner = {"col": col + 1 - 2 * x_lo}
    up_y, down_y = {"col": (col + 2) % COLS}, {"col": (col + COLS - 2) % COLS}
    up, down = {"day": (day + 1) % DAYS}, {"day": (day + DAYS - 1) % DAYS}
    day_up, day_down, day_far = (day + 1) % DAYS, (day + DAYS - 1) % DAYS, (day + 2) % DAYS
    others = (day_down, day_up, day_far)
    offset = (y + 4 - row) % 4
    home = offset == 0
    relay_up = jnp.logical_and(core == 1, offset == 1)
    relay_down = jnp.logical_and(core == 0, offset == 3)
    far = offset == 2
    mine = pl.ds(2 * core, 2)
    theirs = pl.ds(2 - 2 * core, 2)

    barrier = pltpu.get_barrier_semaphore()
    for peer in (sibling, opposite, partner, up_y, down_y, up, down):
        pl.semaphore_signal(barrier, inc=1, device_id=peer, device_id_type=MESH)
    pl.semaphore_wait(barrier, 7)

    pending = []

    def send(k, src, dst, slot, send_slot, peer, when=None):
        def make():
            return pltpu.make_async_remote_copy(
                src_ref=src, dst_ref=dst, send_sem=sent.at[k, send_slot], recv_sem=recv.at[k, slot],
                device_id=peer, device_id_type=MESH)
        if when is None:
            make().start()
        else:
            pl.when(when)(lambda: make().start())
        pending.append((make, when))

    def arrive(k, dst, slot, when=None):
        def wait():
            pltpu.make_async_copy(dst, dst, recv.at[k, slot]).wait()
        if when is None:
            wait()
        else:
            pl.when(when)(wait)

    def span(k):
        return pl.ds(*CHUNKS[k])

    def c_at(k, d, part):
        return near.at[d, span(k), part]

    def r_at(k, d, side, part=pl.ds(0, 4)):
        return full.at[d, span(k), side, part]

    def local(src, dst, k, slot):
        copy = pltpu.make_async_copy(src, dst, here.at[k, slot])
        copy.start()
        return copy

    my_unit = 2 * core + row // 2
    both = pl.ds(0, 2)

    def start_units(k):
        place = near.at[day, span(k), my_unit]
        send(k, unit.at[span(k)], place, 0, 0, opposite)
        local(unit.at[span(k)], place, k, 0).wait()

    def spread_units(k):
        other = 2 * core + 1 - row // 2
        arrive(k, near.at[day, span(k), other], 0)
        send(k, c_at(k, day, mine), c_at(k, day, mine), 1, 1, sibling)
        send(k, c_at(k, day, mine), c_at(k, day, mine), 2, 2, up)
        send(k, c_at(k, day, mine), c_at(k, day, mine), 3, 3, down)

    def seed(k):
        arrive(k, c_at(k, day, theirs), 1)
        everything = near.at[day, span(k)]
        if k % 2 == 0:
            send(k, everything, r_at(k, day, x_lo), 9, 9, up_y, home)
            send(k, everything, r_at(k, day, x_lo), 9, 10, down_y, home)
        else:
            send(k, everything, r_at(k, day, x_lo), 9, 9, partner, home)

        @pl.when(home)
        def _():
            local(everything, r_at(k, day, x_lo), k, 1).wait()

    def near_days(k):
        first, second = pl.ds(2 * core, 1), pl.ds(2 * core + 1, 1)
        arrive(k, c_at(k, day_down, mine), 2)
        send(k, c_at(k, day_down, first), c_at(k, day_down, first), 4, 4, up)
        send(k, c_at(k, day_down, mine), c_at(k, day_down, mine), 6, 6, sibling)
        arrive(k, c_at(k, day_up, mine), 3)
        send(k, c_at(k, day_up, second), c_at(k, day_up, second), 5, 5, down)
        send(k, c_at(k, day_up, mine), c_at(k, day_up, mine), 7, 7, sibling)

    def near_far(k):
        first, second = pl.ds(2 * core, 1), pl.ds(2 * core + 1, 1)
        arrive(k, c_at(k, day_far, first), 4)
        arrive(k, c_at(k, day_far, second), 5)
        send(k, c_at(k, day_far, mine), c_at(k, day_far, mine), 8, 8, sibling)

    def along_day_start(k):
        if k % 2 == 0:
            away = jnp.logical_not(home)
            block = r_at(k, day, x_lo)
            arrive(k, block, 9, away)
            send(k, block, block, 9, 9, up_y, relay_up)
            send(k, block, block, 9, 9, down_y, relay_down)
            send(k, block, block, 10, 11, up)
            send(k, block, block, 11, 12, down)
        else:
            arrive(k, r_at(k, day, 1 - x_lo), 9, home)
            block = r_at(k, day, both)
            send(k, block, block, 10, 11, up, home)
            send(k, block, block, 11, 12, down, home)
            across_y(k, day, 14)

    def across_y(k, d, slot):
        block = r_at(k, d, both)
        send(k, block, block, slot, 2 * slot - 13, up_y, home)
        send(k, block, block, slot, 2 * slot - 12, down_y, home)

    def along_day_near(k):
        if k % 2 == 0:
            block = r_at(k, day, x_lo)
            send(k, block, block, 14, 15, partner)
            part = r_at(k, day_down, x_lo, pl.ds(0, 2))
            arrive(k, r_at(k, day_down, x_lo), 10)
            send(k, part, part, 12, 13, up)
            block = r_at(k, day_down, x_lo)
            send(k, block, block, 15, 16, partner)
            part = r_at(k, day_up, x_lo, pl.ds(2, 2))
            arrive(k, r_at(k, day_up, x_lo), 11)
            send(k, part, part, 13, 14, down)
            block = r_at(k, day_up, x_lo)
            send(k, block, block, 16, 17, partner)
        else:
            part = r_at(k, day_down, 0)
            arrive(k, r_at(k, day_down, both), 10, home)
            send(k, part, part, 12, 13, up, home)
            across_y(k, day_down, 15)
            part = r_at(k, day_up, 1)
            arrive(k, r_at(k, day_up, both), 11, home)
            send(k, part, part, 13, 14, down, home)
            across_y(k, day_up, 16)

    def along_day_far(k):
        if k % 2 == 0:
            arrive(k, r_at(k, day_far, x_lo, pl.ds(0, 2)), 12)
            arrive(k, r_at(k, day_far, x_lo, pl.ds(2, 2)), 13)
            block = r_at(k, day_far, x_lo)
            send(k, block, block, 17, 18, partner)
        else:
            arrive(k, r_at(k, day_far, 0), 12, home)
            arrive(k, r_at(k, day_far, 1), 13, home)
            across_y(k, day_far, 17)

    def relay(k, slots):
        if k % 2 == 1:
            for d, slot in zip((day,) + others, range(14, 18)):
                if slot in slots:
                    block = r_at(k, d, both)
                    near_y = jnp.logical_or(offset == 1, offset == 3)
                    arrive(k, block, slot, near_y)
                    send(k, block, block, slot, 2 * slot - 13, up_y, relay_up)
                    send(k, block, block, slot, 2 * slot - 13, down_y, relay_down)

    def finish(k):
        for d, slot in zip(others, (6, 7, 8)):
            arrive(k, c_at(k, d, theirs), slot)
        for d, slot in zip((day,) + others, range(14, 18)):
            if k % 2 == 0:
                arrive(k, r_at(k, d, 1 - x_lo), slot)
            else:
                arrive(k, r_at(k, d, both), slot, far)

    count = len(CHUNKS)
    for k in range(count):
        start_units(k)
    stages = (
        spread_units,
        seed,
        near_days,
        along_day_start,
        along_day_near,
        near_far,
        along_day_far,
        lambda k: relay(k, range(14, 18)),
        finish,
    )
    for step in range(count + len(stages) - 1):
        for at in reversed(range(len(stages))):
            if 0 <= step - at < count:
                stages[at](step - at)
    for make, when in pending:
        if when is None:
            make().wait_send()
        else:
            pl.when(when)(lambda make=make: make().wait_send())


def gather(unit):
    count = len(CHUNKS)
    channels = unit.shape[1]
    return pl.pallas_call(
        gather_kernel,
        out_shape=(
            jax.ShapeDtypeStruct((DAYS, SLOTS, 4, channels, WIDE), unit.dtype),
            jax.ShapeDtypeStruct((DAYS, SLOTS, 2, 4, channels, WIDE), unit.dtype),
        ),
        in_specs=[pl.BlockSpec(memory_space=pl.ANY)],
        out_specs=(pl.BlockSpec(memory_space=pl.ANY),) * 2,
        scratch_shapes=[
            pltpu.SemaphoreType.DMA((count, 18)),
            pltpu.SemaphoreType.DMA((count, 23)),
            pltpu.SemaphoreType.DMA((count, 2)),
        ],
        compiler_params=pltpu.CompilerParams(collective_id=0, has_side_effects=True),
        name="gather_units",
    )(unit)


def swap8(block):
    return jnp.swapaxes(block, 0, 1)


def correlate_kernel(near, full, table, out, stack, inverse):
    lane = lax.broadcasted_iota(jnp.int32, (64, 2 * WIDE), 1)
    real = (lane // 16) % 2 == 0
    place = (lane // 32) % PACK

    def columns(d, slot):
        return jnp.concatenate([near[d, slot, v] for v in ORDER], axis=0)

    def rows(d, slot):
        return jnp.concatenate([full[d, slot, side, v] for side in range(2) for v in ORDER], axis=0)

    count = jnp.zeros((64, WIDE), jnp.float32)
    for d in range(DAYS):
        count += lax.dot_general(columns(d, 0), rows(d, 0), NT, preferred_element_type=jnp.float32)
    inverse[...] = 1.0 / jnp.maximum(count, 1.0)

    def stack_group(group, _):
        slot = group + 1
        total = None
        for pair in range(DAYS // 2):
            col = jnp.concatenate([columns(2 * pair, slot), columns(2 * pair + 1, slot)], axis=1).astype(jnp.float32)
            row = jnp.concatenate([rows(2 * pair, slot), rows(2 * pair + 1, slot)], axis=1)
            swapped = jnp.where(real, -pltpu.roll(col, 2 * WIDE - 16, 1), pltpu.roll(col, 16, 1))
            parts = []
            for at in range(PACK):
                for side in (col, swapped):
                    parts.append(jnp.where(place == at, side, 0.0).astype(jnp.bfloat16))
            left = jnp.concatenate(parts, axis=0)
            term = lax.dot_general(left, row, NT, preferred_element_type=jnp.float32)
            total = term if total is None else total + term
        total = total.reshape(8, 64, WIDE)
        start = pl.multiple_of(group * 8, 8)
        for at in range(0, 64, 8):
            stack[at : at + 8, pl.ds(start, 8), :] = swap8(total[:, at : at + 8, :])
        return 0

    lax.fori_loop(0, GROUPS, stack_group, 0)

    def lag_group(group, _):
        done = []
        for at in range(8):
            j = group * 8 + at
            values = stack[j]
            high = values.astype(jnp.bfloat16)
            low = (values - high.astype(jnp.float32)).astype(jnp.bfloat16)
            first = jnp.dot(table[...], high, preferred_element_type=jnp.float32)
            second = jnp.dot(table[:WIDE], low, preferred_element_type=jnp.float32)
            lags = (first[:WIDE] + first[WIDE:] + second) * inverse[pl.ds(j, 1), :]
            done.append(lags.T)
        start = pl.multiple_of(group * 8, 8)
        for at in range(0, WIDE, 8):
            out[at : at + 8, pl.ds(start, 8), :] = swap8(jnp.stack([d[at : at + 8] for d in done]))
        return 0

    lax.fori_loop(0, 8, lag_group, 0)


def correlate(near, full, table):
    return pl.pallas_call(
        correlate_kernel,
        out_shape=jax.ShapeDtypeStruct((WIDE, 64, WIDE), jnp.float32),
        in_specs=[pl.BlockSpec(memory_space=pltpu.VMEM)] * 3,
        out_specs=pl.BlockSpec(memory_space=pltpu.VMEM),
        scratch_shapes=[pltpu.VMEM((64, 2 * F, WIDE), jnp.float32), pltpu.VMEM((64, WIDE), jnp.float32)],
        compiler_params=pltpu.CompilerParams(vmem_limit_bytes=56 << 20),
        name="correlate",
    )(near, full, table)


def per_device(spectra, validity):
    table = lax.dynamic_index_in_dim(jnp.asarray(lag_tables()), lax.axis_index("day"), keepdims=False)
    near, full = gather(own_unit(spectra, validity))
    return correlate(near, full, table)


def solution(mesh):
    placed = (P("day", None, ("col", "row"), None), P("day", ("col", "row")))
    return jax.shard_map(
        per_device, mesh=mesh, in_specs=placed, out_specs=P("row", "col", "day"), check_vma=False
    )
```

time: 427 us -> 160 us (0.37)
  waiting for transfers between devices: 287 us -> 0 us
  Pallas kernels: 0 us -> 154 us
  blocking collectives: 48.4 us -> 0 us
  matrix products: 47.3 us -> 0 us
  local copies, waits for them, and re-layouts: 20.8 us -> 3.39 us
  between operations: 13.2 us -> 0.04 us
  other arithmetic: 9.43 us -> 1.79 us
    all_gather x2 -> x0, waiting for transfers between devices: 155 us -> none  [the longest x1 131 us: per_device(): lax.all_gather(col_spec, 'col', axis=2, tiled=True)]
    pallas_call x0 -> x2, Pallas kernels: none -> 154 us  [the longest x1 115 us: gather(): pl.pallas_call(gather_kernel, out_shape=(jax.ShapeDtypeStruct((DAYS, SLOT...]
    reduce_scatter x1 -> x0, waiting for transfers between devices: 132 us -> none  [per_device(): lax.psum_scatter(jnp.einsum('stf,sijf->tij', table, stacked, precision=la...]
    dot_general x3 -> x0, matrix products: 47.3 us -> none  [the longest x1 43.1 us: per_device(): jnp.einsum('stf,sijf->tij', table, stacked, precision=lax.Precision.HIGHEST)]
    all_gather x2 -> x0, blocking collectives: 31.2 us -> none  [the longest x1 24.6 us: per_device(): lax.all_gather(col_flag, 'col', axis=2, tiled=True)]
    psum x1 -> x0, blocking collectives: 17.2 us -> none  [per_device(): lax.psum(local_counts(row_flag, col_flag).astype(jnp.bfloat16), 'day')]
    unnamed x9 -> x1, local copies, waits for them, and re-layouts: 7.92 us -> 0.77 us
    div x1 -> x0, local copies, waits for them, and re-layouts: 5.34 us -> none  [per_device(): jnp.transpose(numerator, (1, 2, 0))]
  transfers between devices with their start and end apart: 3 -> 0, of which waited for: 3 -> 0; matrix products, arithmetic and copies ran while one was open for 2% -> 0% of each run, Pallas kernels for 0% -> 0%
where the time goes in v1:
time: 160 us; the launch traced here: 159 us
  Pallas kernels  154 us (96%)
  local copies, waits for them, and re-layouts  3.39 us (2%)
  other arithmetic  1.79 us (1%)
    pallas_call x1, Pallas kernels, gather(): pl.pallas_call(gather_kernel, out_shape=(jax.ShapeDtypeStruct((DAYS, SLOT...  115 us
    pallas_call x1, Pallas kernels, correlate(): pl.pallas_call(correlate_kernel, out_shape=jax.ShapeDtypeStruct((WIDE, 64...  39.1 us

profile of v1, /device:TPU:16, one launch (start us, length us, event | category | flops | bytes accessed | tf_op | source)
XLA Modules:
  0.0 159.3 jit_solution(9498309961894272)
XLA Ops:
  0.0 0.8 copy.7
  0.8 0.1 copy.8
  0.9 1.1 broadcast_multiply_fusion
  1.9 1.7 %dynamic-slice_bitcast_fusion.table = bf16[256,512]{1,0:T(8,128)(2,1)} fusion(bf16[4,256,512]{2,1,0:T(8,128)(2,1)} %constant.15.clone, s32[]{:T(128)S(6)} %select_n.4), kind=kLoop, calls=%fused_computation.1 | loop fusion | bytes 524292 | tf_op jit(solution)/shard_map/jit(dynamic_index_in_dim)/squeeze | solution.py:343
  3.6 0.2 reshape.7
  3.9 0.3 copy.9
  4.2 0.3 copy.10
  4.5 0.7 pad_maximum_fusion.unit
  5.2 115.0 %gather_units.1 = (bf16[4,65,4,16,128]{4,3,2,1,0:T(8,128)(2,1)}, bf16[4,65,2,4,16,128]{5,4,3,2,1,0:T(8,128)(2,1)}) custom-call(bf16[65,16,128]{2,1,0:T(8,128)(2,1)} %pad_maximum_fusion.unit), custom_call_target="tpu_custom_call" | custom-call | tf_op jit(solution)/shard_map/gather_units/pallas_call | solution.py:251
  120.2 39.1 %correlate.1 = f32[128,64,128]{2,1,0:T(8,128)} custom-call(bf16[4,65,4,16,128]{4,3,2,1,0:T(8,128)(2,1)} %get-tuple-element.7.near, bf16[4,65,2,4,16,128]{5,4,3,2,1,0:T(8,128)(2,1)} %get-tuple-element.8.full, bf16[256,512]{1,0:T(8,128)(2,1)} %dynamic-slice_bitcast_fusion.table), custom_call_target="tpu_custom_call" | custom-call | tf_op jit(solution)/shard_map/correlate/pallas_call | solution.py:331
  (3 shorter events, 0.0 us)

commit v2 on v1

--- a/solution.py
+++ b/solution.py
@@ -2,7 +2,6 @@
 
 import jax
 import jax.numpy as jnp
-import ml_dtypes
 import numpy as np
 from jax import lax
 from jax.experimental import pallas as pl
@@ -28,10 +27,7 @@
     phase = 2.0 * math.pi / (2 * F) * np.mod(lag[:, None] * freq[None, :], 2 * F)
     both = np.stack([np.cos(phase), -np.sin(phase)]) / math.sqrt(F)
     both = both.reshape(2, DAYS, LAGS // DAYS, PACK, GROUPS).transpose(1, 2, 4, 3, 0)
-    both = both.reshape(DAYS, LAGS // DAYS, 2 * F).astype(np.float32)
-    high = both.astype(ml_dtypes.bfloat16)
-    low = (both - high.astype(np.float32)).astype(ml_dtypes.bfloat16)
-    return np.concatenate([high, low], axis=1)
+    return both.reshape(DAYS, LAGS // DAYS, 2 * F).astype(np.float32)
 
 
 def own_unit(spectra, validity):
@@ -44,7 +40,11 @@
     return jnp.concatenate([first[None], packed])
 
 
-def gather_kernel(unit, near, full, recv, sent, here):
+def swap8(block):
+    return jnp.swapaxes(block, 0, 1)
+
+
+def correlate_kernel(unit, tables, out, near, full, stack, partial, exact, table, inverse, recv, sent, here, table_sem):
     row, col, day = lax.axis_index("row"), lax.axis_index("col"), lax.axis_index("day")
     core, x_lo, y = row % 2, col % 2, col // 2
     sibling = {"row": row + 1 - 2 * core}
@@ -62,6 +62,9 @@
     mine = pl.ds(2 * core, 2)
     theirs = pl.ds(2 - 2 * core, 2)
 
+    table_copy = pltpu.make_async_copy(tables.at[day], exact, table_sem)
+    table_copy.start()
+
     barrier = pltpu.get_barrier_semaphore()
     for peer in (sibling, opposite, partner, up_y, down_y, up, down):
         pl.semaphore_signal(barrier, inc=1, device_id=peer, device_id_type=MESH)
@@ -220,7 +223,89 @@
             else:
                 arrive(k, r_at(k, d, both), slot, far)
 
+    lane = lax.broadcasted_iota(jnp.int32, (64, 2 * WIDE), 1)
+    real = (lane // 16) % 2 == 0
+    place = (lane // 32) % PACK
+
+    def columns(d, slot):
+        return jnp.concatenate([near[d, slot, v] for v in ORDER], axis=0)
+
+    def rows(d, slot):
+        return jnp.concatenate([full[d, slot, side, v] for side in range(2) for v in ORDER], axis=0)
+
+    def pair_counts():
+        total = jnp.zeros((64, WIDE), jnp.float32)
+        for d in range(DAYS):
+            total += lax.dot_general(columns(d, 0), rows(d, 0), NT, preferred_element_type=jnp.float32)
+        inverse[...] = 1.0 / jnp.maximum(total, 1.0)
+
+    def stack_group(group):
+        slot = group + 1
+        total = None
+        for pair in range(DAYS // 2):
+            col = jnp.concatenate([columns(2 * pair, slot), columns(2 * pair + 1, slot)], axis=1).astype(jnp.float32)
+            row = jnp.concatenate([rows(2 * pair, slot), rows(2 * pair + 1, slot)], axis=1)
+            swapped = jnp.where(real, -pltpu.roll(col, 2 * WIDE - 16, 1), pltpu.roll(col, 16, 1))
+            parts = []
+            for at in range(PACK):
+                for side in (col, swapped):
+                    parts.append(jnp.where(place == at, side, 0.0).astype(jnp.bfloat16))
+            left = jnp.concatenate(parts, axis=0)
+            term = lax.dot_general(left, row, NT, preferred_element_type=jnp.float32)
+            total = term if total is None else total + term
+        total = total.reshape(8, 64, WIDE)
+        start = pl.multiple_of(group * 8, 8)
+        for at in range(0, 64, 8):
+            stack[at : at + 8, pl.ds(start, 8), :] = swap8(total[:, at : at + 8, :])
+
+    def split_table():
+        table_copy.wait()
+        high = exact[...].astype(jnp.bfloat16)
+        table[:WIDE] = high
+        table[WIDE:] = (exact[...] - high.astype(jnp.float32)).astype(jnp.bfloat16)
+
+    def half_lags(j, half):
+        span = pl.ds(half * F, F)
+        values = stack[j, span, :]
+        high = values.astype(jnp.bfloat16)
+        low = (values - high.astype(jnp.float32)).astype(jnp.bfloat16)
+        first = jnp.dot(table[:, span], high, preferred_element_type=jnp.float32)
+        second = jnp.dot(table[:WIDE, span], low, preferred_element_type=jnp.float32)
+        return first[:WIDE] + first[WIDE:] + second
+
+    def first_half(group):
+        for at in range(8):
+            partial[group * 8 + at] = half_lags(group * 8 + at, 0)
+
+    def second_half(group):
+        done = []
+        for at in range(8):
+            j = group * 8 + at
+            done.append(((partial[j] + half_lags(j, 1)) * inverse[pl.ds(j, 1), :]).T)
+        start = pl.multiple_of(group * 8, 8)
+        for at in range(0, WIDE, 8):
+            out[at : at + 8, pl.ds(start, 8), :] = swap8(jnp.stack([d[at : at + 8] for d in done]))
+
+    def repeat(body, first, times):
+        def step(at, _):
+            body(at)
+            return 0
+
+        lax.fori_loop(first, first + times, step, 0)
+
     count = len(CHUNKS)
+    work = []
+
+    def ready(k):
+        if k == 0:
+            work.append(pair_counts)
+        for at in range(0, GROUPS // count, 2):
+            work.append(lambda first=k * GROUPS // count + at: repeat(stack_group, first, 2))
+        if k == count // 2 - 1:
+            work.append(split_table)
+            for at in range(0, 8, 2):
+                work.append(lambda first=at: repeat(first_half, first, 2))
+
     for k in range(count):
         start_units(k)
     stages = (
@@ -238,6 +323,13 @@
         for at in reversed(range(len(stages))):
             if 0 <= step - at < count:
                 stages[at](step - at)
+                if work:
+                    work.pop(0)()
+        if 0 <= step + 1 - len(stages) < count:
+            ready(step + 1 - len(stages))
+    for item in work:
+        item()
+    repeat(second_half, 0, 8)
     for make, when in pending:
         if when is None:
             make().wait_send()
@@ -245,104 +337,35 @@
             pl.when(when)(lambda make=make: make().wait_send())
 
 
-def gather(unit):
+def correlate(unit, tables):
     count = len(CHUNKS)
     channels = unit.shape[1]
+    vmem = pl.BlockSpec(memory_space=pltpu.VMEM)
     return pl.pallas_call(
-        gather_kernel,
-        out_shape=(
-            jax.ShapeDtypeStruct((DAYS, SLOTS, 4, channels, WIDE), unit.dtype),
-            jax.ShapeDtypeStruct((DAYS, SLOTS, 2, 4, channels, WIDE), unit.dtype),
-        ),
-        in_specs=[pl.BlockSpec(memory_space=pl.ANY)],
-        out_specs=(pl.BlockSpec(memory_space=pl.ANY),) * 2,
+        correlate_kernel,
+        out_shape=jax.ShapeDtypeStruct((WIDE, 64, WIDE), jnp.float32),
+        in_specs=[vmem, pl.BlockSpec(memory_space=pl.ANY)],
+        out_specs=vmem,
         scratch_shapes=[
+            pltpu.VMEM((DAYS, SLOTS, 4, channels, WIDE), unit.dtype),
+            pltpu.VMEM((DAYS, SLOTS, 2, 4, channels, WIDE), unit.dtype),
+            pltpu.VMEM((64, 2 * F, WIDE), jnp.float32),
+            pltpu.VMEM((64, WIDE, WIDE), jnp.float32),
+            pltpu.VMEM((WIDE, 2 * F), jnp.float32),
+            pltpu.VMEM((2 * WIDE, 2 * F), jnp.bfloat16),
+            pltpu.VMEM((64, WIDE), jnp.float32),
             pltpu.SemaphoreType.DMA((count, 18)),
             pltpu.SemaphoreType.DMA((count, 23)),
             pltpu.SemaphoreType.DMA((count, 2)),
+            pltpu.SemaphoreType.DMA,
         ],
-        compiler_params=pltpu.CompilerParams(collective_id=0, has_side_effects=True),
-        name="gather_units",
-    )(unit)
-
-
-def swap8(block):
-    return jnp.swapaxes(block, 0, 1)
-
-
-def correlate_kernel(near, full, table, out, stack, inverse):
-    lane = lax.broadcasted_iota(jnp.int32, (64, 2 * WIDE), 1)
-    real = (lane // 16) % 2 == 0
-    place = (lane // 32) % PACK
-
-    def columns(d, slot):
-        return jnp.concatenate([near[d, slot, v] for v in ORDER], axis=0)
-
-    def rows(d, slot):
-        return jnp.concatenate([full[d, slot, side, v] for side in range(2) for v in ORDER], axis=0)
-
-    count = jnp.zeros((64, WIDE), jnp.float32)
-    for d in range(DAYS):
-        count += lax.dot_general(columns(d, 0), rows(d, 0), NT, preferred_element_type=jnp.float32)
-    inverse[...] = 1.0 / jnp.maximum(count, 1.0)
-
-    def stack_group(group, _):
-        slot = group + 1
-        total = None
-        for pair in range(DAYS // 2):
-            col = jnp.concatenate([columns(2 * pair, slot), columns(2 * pair + 1, slot)], axis=1).astype(jnp.float32)
-            row = jnp.concatenate([rows(2 * pair, slot), rows(2 * pair + 1, slot)], axis=1)
-            swapped = jnp.where(real, -pltpu.roll(col, 2 * WIDE - 16, 1), pltpu.roll(col, 16, 1))
-            parts = []
-            for at in range(PACK):
-                for side in (col, swapped):
-                    parts.append(jnp.where(place == at, side, 0.0).astype(jnp.bfloat16))
-            left = jnp.concatenate(parts, axis=0)
-            term = lax.dot_general(left, row, NT, preferred_element_type=jnp.float32)
-            total = term if total is None else total + term
-        total = total.reshape(8, 64, WIDE)
-        start = pl.multiple_of(group * 8, 8)
-        for at in range(0, 64, 8):
-            stack[at : at + 8, pl.ds(start, 8), :] = swap8(total[:, at : at + 8, :])
-        return 0
-
-    lax.fori_loop(0, GROUPS, stack_group, 0)
-
-    def lag_group(group, _):
-        done = []
-        for at in range(8):
-            j = group * 8 + at
-            values = stack[j]
-            high = values.astype(jnp.bfloat16)
-            low = (values - high.astype(jnp.float32)).astype(jnp.bfloat16)
-            first = jnp.dot(table[...], high, preferred_element_type=jnp.float32)
-            second = jnp.dot(table[:WIDE], low, preferred_element_type=jnp.float32)
-            lags = (first[:WIDE] + first[WIDE:] + second) * inverse[pl.ds(j, 1), :]
-            done.append(lags.T)
-        start = pl.multiple_of(group * 8, 8)
-        for at in range(0, WIDE, 8):
-            out[at : at + 8, pl.ds(start, 8), :] = swap8(jnp.stack([d[at : at + 8] for d in done]))
-        return 0
-
-    lax.fori_loop(0, 8, lag_group, 0)
-
-
-def correlate(near, full, table):
-    return pl.pallas_call(
-        correlate_kernel,
-        out_shape=jax.ShapeDtypeStruct((WIDE, 64, WIDE), jnp.float32),
-        in_specs=[pl.BlockSpec(memory_space=pltpu.VMEM)] * 3,
-        out_specs=pl.BlockSpec(memory_space=pltpu.VMEM),
-        scratch_shapes=[pltpu.VMEM((64, 2 * F, WIDE), jnp.float32), pltpu.VMEM((64, WIDE), jnp.float32)],
-        compiler_params=pltpu.CompilerParams(vmem_limit_bytes=56 << 20),
+        compiler_params=pltpu.CompilerParams(collective_id=0, has_side_effects=True, vmem_limit_bytes=52 << 20),
         name="correlate",
-    )(near, full, table)
+    )(unit, tables)
 
 
 def per_device(spectra, validity):
-    table = lax.dynamic_index_in_dim(jnp.asarray(lag_tables()), lax.axis_index("day"), keepdims=False)
-    near, full = gather(own_unit(spectra, validity))
-    return correlate(near, full, table)
+    return correlate(own_unit(spectra, validity), jnp.asarray(lag_tables()))
 
 
 def solution(mesh):

time: 160 us -> 123 us (0.77)
  Pallas kernels: 154 us -> 115 us
  local copies, waits for them, and re-layouts: 3.39 us -> 6.6 us
    pallas_call x1 -> x0, Pallas kernels: 115 us -> none  [gather(): pl.pallas_call(gather_kernel, out_shape=(jax.ShapeDtypeStruct((DAYS, SLOT...]
    pallas_call x1, Pallas kernels: 39.1 us -> 115 us  [correlate(): pl.pallas_call(correlate_kernel, out_shape=jax.ShapeDtypeStruct((WIDE, 64...]
    unnamed x1 -> x4, local copies, waits for them, and re-layouts: 0.77 us -> 5.65 us
    squeeze x1 -> x0, local copies, waits for them, and re-layouts: 1.68 us -> none  [per_device(): lax.dynamic_index_in_dim(jnp.asarray(lag_tables()), lax.axis_index('day')...]
where the time goes in v2:
time: 123 us
  Pallas kernels  115 us (93%)
  local copies, waits for them, and re-layouts  6.6 us (5%)
    pallas_call x1, Pallas kernels, correlate(): pl.pallas_call(correlate_kernel, out_shape=jax.ShapeDtypeStruct((WIDE, 64...  115 us
    unnamed x4, local copies, waits for them, and re-layouts  5.65 us

profile of v2, /device:TPU:16, one launch (start us, length us, event | category | flops | bytes accessed | tf_op | source)
XLA Modules:
  0.0 122.5 jit_solution(7617463802416232800)
XLA Ops:
  0.0 0.0 copy-start
  0.0 0.9 copy.7
  0.9 0.1 copy.8
  1.0 1.1 broadcast_multiply_fusion
  2.0 0.2 reshape.7
  2.3 0.3 copy.9
  2.6 0.3 copy.10
  2.9 0.0 copy-done
  2.9 114.8 %correlate.1 = f32[128,64,128]{2,1,0:T(8,128)} custom-call(bf16[65,16,128]{2,1,0:T(8,128)(2,1)S(1)} %pad_maximum_fusion.unit, f32[4,128,512]{2,1,0:T(8,128)S(1)} %copy-done), custom_call_target="tpu_custom_call" | custom-call | tf_op jit(solution)/shard_map/correlate/pallas_call | solution.py:344
  117.7 4.8 %copy.12 = f32[128,64,128]{2,1,0:T(8,128)} copy(f32[128,64,128]{2,1,0:T(8,128)} %correlate.1) | data formatting | bytes 8388608
  (4 shorter events, 0.0 us)
Async XLA Ops:
  0.0 2.9 %copy-start = (f32[4,128,512]{2,1,0:T(8,128)S(1)}, f32[4,128,512]{2,1,0:T(8,128)}, u32[]{:S(2)}) copy-start(f32[4,128,512]{2,1,0:T(8,128)} %constant.5.clone.tables) | copy-start | bytes 3145732

commit v3 on v2

v3 whole, which is shorter than its diff:
```python
import math

import jax
import jax.numpy as jnp
import numpy as np
from jax import lax
from jax.experimental import pallas as pl
from jax.experimental.pallas import tpu as pltpu
from jax.sharding import PartitionSpec as P

F = 256
LAGS = 512
ROWS, COLS, DAYS = 4, 8, 4
PACK = 4
GROUPS = F // PACK
SLOTS = GROUPS + 1
WIDE = 128
SIZES = (6, 9, 8, 10, 8, 8, 8, 8)
MIDDLE = 3
ORDER = (0, 2, 1, 3)
MESH = pl.DeviceIdType.MESH
NT = (((1,), (1,)), ((), ()))


def lag_tables():
    lag = np.arange(LAGS) - LAGS // 2
    freq = np.arange(F)
    phase = 2.0 * math.pi / (2 * F) * np.mod(lag[:, None] * freq[None, :], 2 * F)
    both = np.stack([np.cos(phase), -np.sin(phase)]) / math.sqrt(F)
    both = both.reshape(2, DAYS, LAGS // DAYS, PACK, GROUPS).transpose(1, 2, 4, 3, 0)
    return both.reshape(DAYS, LAGS // DAYS, 2 * F).astype(np.float32)


def own_unit(spectra, validity):
    windows, _, channels, _ = spectra.shape
    flags = validity.astype(jnp.bfloat16)
    cleaned = spectra * flags[:, None, :, None]
    split = cleaned.reshape(windows, 2, channels, PACK, GROUPS)
    packed = jnp.transpose(split, (4, 2, 3, 1, 0)).reshape(GROUPS, channels, WIDE)
    first = jnp.pad(flags.T, ((0, 0), (0, WIDE - windows)))
    return jnp.concatenate([first[None], packed])


def swap8(block):
    return jnp.swapaxes(block, 0, 1)


def correlate_kernel(unit, tables, out, near, full, stack, partial, exact, table, inverse, recv, sent, here, table_sem):
    row, col, day = lax.axis_index("row"), lax.axis_index("col"), lax.axis_index("day")
    core, x_hi, x_lo, y = row % 2, row // 2, col % 2, col // 2
    sibling = {"row": row + 1 - 2 * core}
    opposite = {"row": (row + 2) % ROWS}
    partner = {"col": col + 1 - 2 * x_lo}
    up_y, down_y = {"col": (col + 2) % COLS}, {"col": (col + COLS - 2) % COLS}
    days = [{"day": (day + step) % DAYS} for step in range(DAYS)]
    offset = (y + 4 - row) % 4
    home = offset == 0
    away = offset != 0
    beside = jnp.logical_or(offset == 1, offset == 3)
    far = offset == 2
    relay_up = jnp.logical_and(core == 1, offset == 1)
    relay_down = jnp.logical_and(core == 0, offset == 3)
    home_chip = x_hi == y // 2
    other_chip = x_hi != y // 2
    home_sibling = jnp.logical_and(home_chip, away)

    barrier = pltpu.get_barrier_semaphore()
    for peer in (sibling, opposite, partner, up_y, down_y, *days[1:]):
        pl.semaphore_signal(barrier, inc=1, device_id=peer, device_id_type=MESH)

    table_copy = pltpu.make_async_copy(tables.at[day], exact, table_sem)
    table_copy.start()

    count = len(SIZES)
    spans = [pl.ds(sum(SIZES[:k]), SIZES[k]) for k in range(count)]
    mine, theirs = pl.ds(2 * core, 2), pl.ds(2 - 2 * core, 2)
    all_units, both, later = pl.ds(0, 4), pl.ds(0, 2), pl.ds(1, DAYS - 1)
    pending = [[] for _ in range(count)]

    def act(when, body):
        if when is None:
            body()
        else:
            pl.when(when)(body)

    def send(k, src, dst, slot, peer, when=None, extra=0):
        def make():
            return pltpu.make_async_remote_copy(
                src_ref=src, dst_ref=dst, send_sem=sent.at[k, slot + extra], recv_sem=recv.at[k, slot],
                device_id=peer, device_id_type=MESH)

        act(when, lambda: make().start())
        pending[k].append((make, when))

    def arrive(k, dst, slot, when=None):
        act(when, lambda: pltpu.make_async_copy(dst, dst, recv.at[k, slot]).wait())

    def sent_all(k):
        for make, when in pending[k]:
            act(when, lambda make=make: make().wait_send())

    def n_at(k, d, part=all_units):
        return near.at[d, spans[k], part]

    def f_at(k, d, side, part=all_units):
        return full.at[d, spans[k], side, part]

    def day_sends(k, block, place, slot, when=None):
        for step in (1, 3, 2):
            send(k, block, place(DAYS - step), slot + step - 1, days[step], when)

    def day_arrivals(k, place, slot, when=None):
        for step in (1, 3, 2):
            arrive(k, place(DAYS - step), slot + step - 1, when)

    def start_units(k):
        place = near.at[0, spans[k], 2 * core + x_hi]
        send(k, unit.at[spans[k]], place, 0, opposite)
        copy = pltpu.make_async_copy(unit.at[spans[k]], place, here.at[k, 0])
        copy.start()
        return copy

    def spread_units(k):
        arrive(k, near.at[0, spans[k], 2 * core + 1 - x_hi], 0)
        copies[k].wait()
        block = n_at(k, 0, mine)
        send(k, block, block, 1, sibling)
        day_sends(k, block, lambda d: n_at(k, d, mine), 2, other_chip)

    def first_spread(k):
        arrive(k, n_at(k, 0, theirs), 1)
        block, place = n_at(k, 0), f_at(k, 0, x_lo)

        @pl.when(home)
        def _():
            copy = pltpu.make_async_copy(block, place, here.at[k, 1])
            copy.start()
            copy.wait()

        if k % 2 == 0:
            send(k, block, place, 6, up_y, home)
            send(k, block, place, 6, down_y, home, extra=6)
        else:
            send(k, block, place, 6, partner, home)

    def own_day(k):
        if k % 2 == 0:
            block = f_at(k, 0, x_lo)
            arrive(k, block, 6, away)
            send(k, block, block, 6, up_y, relay_up)
            send(k, block, block, 6, down_y, relay_down)
            day_sends(k, block, lambda d: f_at(k, d, x_lo), 7)
            send(k, block, block, 10, partner)
        else:
            arrive(k, f_at(k, 0, 1 - x_lo), 6, home)
            block = f_at(k, 0, both)
            day_sends(k, block, lambda d: f_at(k, d, both), 7, home)
            send(k, block, block, 10, up_y, home)
            send(k, block, block, 10, down_y, home, extra=3)

    def later_days(k):
        day_arrivals(k, lambda d: n_at(k, d, mine), 2, other_chip)
        block = n_at(k, later, mine)
        send(k, block, block, 5, sibling, other_chip)
        if k % 2 == 0:
            day_arrivals(k, lambda d: f_at(k, d, x_lo), 7)
            block = f_at(k, later, x_lo)
            send(k, block, block, 11, partner)
        else:
            day_arrivals(k, lambda d: f_at(k, d, both), 7, home)
            block = f_at(k, later, both)
            send(k, block, block, 11, up_y, home)
            send(k, block, block, 11, down_y, home, extra=3)
        block, place = f_at(k, later, x_lo), n_at(k, later)
        send(k, block, place, 5, sibling, home)
        act(home, lambda: pltpu.make_async_copy(block, place, here.at[k, 0]).start())

    def relay_own(k):
        if k % 2 == 1:
            relay(k, f_at(k, 0, both), 10)

    def relay_later(k):
        if k % 2 == 1:
            relay(k, f_at(k, later, both), 11)

    def relay(k, block, slot):
        arrive(k, block, slot, beside)
        send(k, block, block, slot, up_y, relay_up)
        send(k, block, block, slot, down_y, relay_down)

    def finish(k):
        arrive(k, n_at(k, later, theirs), 5, other_chip)
        arrive(k, n_at(k, later), 5, home_sibling)
        act(home, lambda: pltpu.make_async_copy(f_at(k, later, x_lo), n_at(k, later), here.at[k, 0]).wait())
        if k % 2 == 0:
            arrive(k, f_at(k, 0, 1 - x_lo), 10)
            arrive(k, f_at(k, later, 1 - x_lo), 11)
        else:
            arrive(k, f_at(k, 0, both), 10, far)
            arrive(k, f_at(k, later, both), 11, far)

    lane = lax.broadcasted_iota(jnp.int32, (64, 2 * WIDE), 1)
    real = (lane // 16) % 2 == 0
    place = (lane // 32) % PACK

    def columns(d, slot):
        return jnp.concatenate([near[d, slot, v] for v in ORDER], axis=0)

    def rows(d, slot):
        return jnp.concatenate([full[d, slot, side, v] for side in range(2) for v in ORDER], axis=0)

    def pair_counts():
        total = jnp.zeros((64, WIDE), jnp.float32)
        for d in range(DAYS):
            total += lax.dot_general(columns(d, 0), rows(d, 0), NT, preferred_element_type=jnp.float32)
        inverse[...] = 1.0 / jnp.maximum(total, 1.0)

    def stack_group(group):
        slot = group + 1
        total = None
        for pair in range(DAYS // 2):
            col = jnp.concatenate([columns(2 * pair, slot), columns(2 * pair + 1, slot)], axis=1).astype(jnp.float32)
            row = jnp.concatenate([rows(2 * pair, slot), rows(2 * pair + 1, slot)], axis=1)
            swapped = jnp.where(real, -pltpu.roll(col, 2 * WIDE - 16, 1), pltpu.roll(col, 16, 1))
            parts = []
            for at in range(PACK):
                for side in (col, swapped):
                    parts.append(jnp.where(place == at, side, 0.0).astype(jnp.bfloat16))
            left = jnp.concatenate(parts, axis=0)
            term = lax.dot_general(left, row, NT, preferred_element_type=jnp.float32)
            total = term if total is None else total + term
        total = total.reshape(8, 64, WIDE)
        start = pl.multiple_of(group * 8, 8)
        for at in range(0, 64, 8):
            stack[at : at + 8, pl.ds(start, 8), :] = swap8(total[:, at : at + 8, :])

    def split_table():
        table_copy.wait()
        high = exact[...].astype(jnp.bfloat16)
        table[:WIDE] = high
        table[WIDE:] = (exact[...] - high.astype(jnp.float32)).astype(jnp.bfloat16)

    def half_lags(j, half):
        span = pl.ds(half * F, F)
        values = stack[j, span, :]
        high = values.astype(jnp.bfloat16)
        low = (values - high.astype(jnp.float32)).astype(jnp.bfloat16)
        first = jnp.dot(table[:, span], high, preferred_element_type=jnp.float32)
        second = jnp.dot(table[:WIDE, span], low, preferred_element_type=jnp.float32)
        return first[:WIDE] + first[WIDE:] + second

    def first_half(group):
        for at in range(8):
            partial[group * 8 + at] = half_lags(group * 8 + at, 0)

    def second_half(group):
        done = []
        for at in range(8):
            j = group * 8 + at
            done.append(((partial[j] + half_lags(j, 1)) * inverse[pl.ds(j, 1), :]).T)
        start = pl.multiple_of(group * 8, 8)
        for at in range(0, WIDE, 8):
            out[at : at + 8, pl.ds(start, 8), :] = swap8(jnp.stack([d[at : at + 8] for d in done]))

    def repeat(body, first, times):
        def step(at, _):
            body(at)
            return 0

        lax.fori_loop(first, first + times, step, 0)

    work = []

    def ready(k):
        if k == 0:
            work.append(pair_counts)
        first, last = max(sum(SIZES[:k]) - 1, 0), sum(SIZES[: k + 1]) - 1
        for at in range(first, last, 2):
            work.append(lambda at=at: repeat(stack_group, at, min(2, last - at)))
        if k == MIDDLE:
            work.append(split_table)
            for at in range(0, 8, 2):
                work.append(lambda first=at: repeat(first_half, first, 2))

    pl.semaphore_wait(barrier, 8)
    copies = [start_units(k) for k in range(count)]
    stages = (spread_units, first_spread, own_day, later_days, relay_own, relay_later, finish)
    for step in range(count + len(stages) - 1):
        for at in reversed(range(len(stages))):
            if 0 <= step - at < count:
                stages[at](step - at)
                if work:
                    work.pop(0)()
        done = step + 1 - len(stages)
        if 0 <= done < count:
            ready(done)
        if 0 < done < count:
            sent_all(done - 1)
    for item in work:
        item()
    repeat(second_half, 0, 8)
    sent_all(count - 1)


def correlate(unit, tables):
    count = len(SIZES)
    channels = unit.shape[1]
    vmem = pl.BlockSpec(memory_space=pltpu.VMEM)
    return pl.pallas_call(
        correlate_kernel,
        out_shape=pltpu.VMEM((WIDE, 64, WIDE), jnp.float32),
        in_specs=[vmem, pl.BlockSpec(memory_space=pl.ANY)],
        out_specs=vmem,
        scratch_shapes=[
            pltpu.VMEM((DAYS, SLOTS, 4, channels, WIDE), unit.dtype),
            pltpu.VMEM((DAYS, SLOTS, 2, 4, channels, WIDE), unit.dtype),
            pltpu.VMEM((64, 2 * F, WIDE), jnp.float32),
            pltpu.VMEM((64, WIDE, WIDE), jnp.float32),
            pltpu.VMEM((WIDE, 2 * F), jnp.float32),
            pltpu.VMEM((2 * WIDE, 2 * F), jnp.bfloat16),
            pltpu.VMEM((64, WIDE), jnp.float32),
            pltpu.SemaphoreType.DMA((count, 12)),
            pltpu.SemaphoreType.DMA((count, 15)),
            pltpu.SemaphoreType.DMA((count, 2)),
            pltpu.SemaphoreType.DMA,
        ],
        compiler_params=pltpu.CompilerParams(collective_id=0, has_side_effects=True, vmem_limit_bytes=44 << 20),
        name="correlate",
    )(unit, tables)


def per_device(spectra, validity):
    return correlate(own_unit(spectra, validity), jnp.asarray(lag_tables()))


def solution(mesh):
    placed = (P("day", None, ("col", "row"), None), P("day", ("col", "row")))
    return jax.shard_map(
        per_device, mesh=mesh, in_specs=placed, out_specs=P("row", "col", "day"), check_vma=False
    )
```

time: 123 us -> 134 us (1.089)
  Pallas kernels: 115 us -> 128 us
  local copies, waits for them, and re-layouts: 6.6 us -> 3.82 us
    pallas_call x1, Pallas kernels: 115 us -> 128 us  [correlate(): pl.pallas_call(correlate_kernel, out_shape=pltpu.VMEM((WIDE, 64, WIDE), j...]
    unnamed x4, local copies, waits for them, and re-layouts: 5.65 us -> 2.87 us
where the time goes in v3:
time: 134 us; the launch traced here: 133 us
  Pallas kernels  128 us (96%)
  local copies, waits for them, and re-layouts  3.82 us (3%)
    pallas_call x1, Pallas kernels, correlate(): pl.pallas_call(correlate_kernel, out_shape=pltpu.VMEM((WIDE, 64, WIDE), j...  128 us
    unnamed x4, local copies, waits for them, and re-layouts  2.87 us

profile of v3, /device:TPU:16, one launch (start us, length us, event | category | flops | bytes accessed | tf_op | source)
XLA Modules:
  0.0 133.4 jit_solution(15466862966170519950)
XLA Ops:
  0.0 0.0 copy-start
  0.0 0.9 copy.7
  0.9 0.1 copy.8
  1.0 1.1 broadcast_multiply_fusion
  2.0 0.2 reshape.7
  2.3 0.3 copy.9
  2.6 0.3 copy.10
  2.9 0.0 copy-done
  2.9 128.4 %correlate.1 = f32[128,64,128]{2,1,0:T(8,128)S(1)} custom-call(bf16[65,16,128]{2,1,0:T(8,128)(2,1)S(1)} %pad_maximum_fusion.unit, f32[4,128,512]{2,1,0:T(8,128)S(1)} %copy-done), custom_call_target="tpu_custom_call" | custom-call | tf_op jit(solution)/shard_map/correlate/pallas_call | solution.py:309
  131.4 2.0 %copy.12 = f32[128,64,128]{2,1,0:T(8,128)} copy(f32[128,64,128]{2,1,0:T(8,128)S(1)} %correlate.1) | data formatting | bytes 8388608
  (4 shorter events, 0.0 us)
Async XLA Ops:
  0.0 2.9 %copy-start = (f32[4,128,512]{2,1,0:T(8,128)S(1)}, f32[4,128,512]{2,1,0:T(8,128)}, u32[]{:S(2)}) copy-start(f32[4,128,512]{2,1,0:T(8,128)} %constant.5.clone.tables) | copy-start | bytes 3145732

commit v4 on v3

--- a/solution.py
+++ b/solution.py
@@ -15,8 +15,10 @@
 GROUPS = F // PACK
 SLOTS = GROUPS + 1
 WIDE = 128
-SIZES = (6, 9, 8, 10, 8, 8, 8, 8)
-MIDDLE = 3
+CHUNKS = "A5 B5 A6 B6 A6 B5 A5 B5 A5 B5 A5 B4 A3"
+KINDS = [name[0] for name in CHUNKS.split()]
+SIZES = [int(name[1:]) for name in CHUNKS.split()]
+IDLE = (1, 1, 2, 1, 0, 1)
 ORDER = (0, 2, 1, 3)
 MESH = pl.DeviceIdType.MESH
 NT = (((1,), (1,)), ((), ()))
@@ -137,14 +139,14 @@
             copy.start()
             copy.wait()
 
-        if k % 2 == 0:
+        if KINDS[k] == "A":
             send(k, block, place, 6, up_y, home)
             send(k, block, place, 6, down_y, home, extra=6)
         else:
             send(k, block, place, 6, partner, home)
 
     def own_day(k):
-        if k % 2 == 0:
+        if KINDS[k] == "A":
             block = f_at(k, 0, x_lo)
             arrive(k, block, 6, away)
             send(k, block, block, 6, up_y, relay_up)
@@ -162,26 +164,32 @@
         day_arrivals(k, lambda d: n_at(k, d, mine), 2, other_chip)
         block = n_at(k, later, mine)
         send(k, block, block, 5, sibling, other_chip)
-        if k % 2 == 0:
+        if KINDS[k] == "A":
             day_arrivals(k, lambda d: f_at(k, d, x_lo), 7)
             block = f_at(k, later, x_lo)
             send(k, block, block, 11, partner)
         else:
             day_arrivals(k, lambda d: f_at(k, d, both), 7, home)
-            block = f_at(k, later, both)
-            send(k, block, block, 11, up_y, home)
-            send(k, block, block, 11, down_y, home, extra=3)
+            if KINDS[k] == "B":
+                block = f_at(k, later, both)
+                send(k, block, block, 11, up_y, home)
+                send(k, block, block, 11, down_y, home, extra=3)
         block, place = f_at(k, later, x_lo), n_at(k, later)
         send(k, block, place, 5, sibling, home)
         act(home, lambda: pltpu.make_async_copy(block, place, here.at[k, 0]).start())
 
     def relay_own(k):
-        if k % 2 == 1:
+        if KINDS[k] != "A":
             relay(k, f_at(k, 0, both), 10)
+        if KINDS[k] == "M":
+            day_sends(k, f_at(k, 0, both), lambda d: f_at(k, d, both), 7, beside)
 
     def relay_later(k):
-        if k % 2 == 1:
+        if KINDS[k] == "B":
             relay(k, f_at(k, later, both), 11)
+        if KINDS[k] == "M":
+            arrive(k, f_at(k, 0, both), 10, far)
+            day_sends(k, f_at(k, 0, both), lambda d: f_at(k, d, both), 7, far)
 
     def relay(k, block, slot):
         arrive(k, block, slot, beside)
@@ -192,16 +200,19 @@
         arrive(k, n_at(k, later, theirs), 5, other_chip)
         arrive(k, n_at(k, later), 5, home_sibling)
         act(home, lambda: pltpu.make_async_copy(f_at(k, later, x_lo), n_at(k, later), here.at[k, 0]).wait())
-        if k % 2 == 0:
+        if KINDS[k] == "A":
             arrive(k, f_at(k, 0, 1 - x_lo), 10)
             arrive(k, f_at(k, later, 1 - x_lo), 11)
-        else:
+        elif KINDS[k] == "B":
             arrive(k, f_at(k, 0, both), 10, far)
             arrive(k, f_at(k, later, both), 11, far)
+        else:
+            day_arrivals(k, lambda d: f_at(k, d, both), 7, away)
 
     lane = lax.broadcasted_iota(jnp.int32, (64, 2 * WIDE), 1)
     real = (lane // 16) % 2 == 0
-    place = (lane // 32) % PACK
+    place = (lax.broadcasted_iota(jnp.int32, (1, 2 * WIDE), 1) // 32) % PACK
+    masks = [jnp.where(place == at, 1.0, 0.0).astype(jnp.bfloat16) for at in range(PACK)]
 
     def columns(d, slot):
         return jnp.concatenate([near[d, slot, v] for v in ORDER], axis=0)
@@ -219,18 +230,16 @@
         slot = group + 1
         total = None
         for pair in range(DAYS // 2):
-            col = jnp.concatenate([columns(2 * pair, slot), columns(2 * pair + 1, slot)], axis=1).astype(jnp.float32)
+            col = jnp.concatenate([columns(2 * pair, slot), columns(2 * pair + 1, slot)], axis=1)
             row = jnp.concatenate([rows(2 * pair, slot), rows(2 * pair + 1, slot)], axis=1)
-            swapped = jnp.where(real, -pltpu.roll(col, 2 * WIDE - 16, 1), pltpu.roll(col, 16, 1))
-            parts = []
-            for at in range(PACK):
-                for side in (col, swapped):
-                    parts.append(jnp.where(place == at, side, 0.0).astype(jnp.bfloat16))
-            left = jnp.concatenate(parts, axis=0)
+            wide = col.astype(jnp.float32)
+            swapped = jnp.where(real, -pltpu.roll(wide, 2 * WIDE - 16, 1), pltpu.roll(wide, 16, 1))
+            swapped = swapped.astype(jnp.bfloat16)
+            left = jnp.concatenate([side * mask for mask in masks for side in (col, swapped)], axis=0)
             term = lax.dot_general(left, row, NT, preferred_element_type=jnp.float32)
             total = term if total is None else total + term
         total = total.reshape(8, 64, WIDE)
-        start = pl.multiple_of(group * 8, 8)
+        start = group * 8
         for at in range(0, 64, 8):
             stack[at : at + 8, pl.ds(start, 8), :] = swap8(total[:, at : at + 8, :])
 
@@ -275,19 +284,20 @@
         if k == 0:
             work.append(pair_counts)
         first, last = max(sum(SIZES[:k]) - 1, 0), sum(SIZES[: k + 1]) - 1
-        for at in range(first, last, 2):
-            work.append(lambda at=at: repeat(stack_group, at, min(2, last - at)))
-        if k == MIDDLE:
+        work.append(lambda: [stack_group(at) for at in range(first, last)])
+        if last == GROUPS // 2:
             work.append(split_table)
             for at in range(0, 8, 2):
                 work.append(lambda first=at: repeat(first_half, first, 2))
 
     pl.semaphore_wait(barrier, 8)
     copies = [start_units(k) for k in range(count)]
-    stages = (spread_units, first_spread, own_day, later_days, relay_own, relay_later, finish)
+    stages = [spread_units]
+    for idle, stage in zip(IDLE, (first_spread, own_day, later_days, relay_own, relay_later, finish)):
+        stages += [None] * idle + [stage]
     for step in range(count + len(stages) - 1):
         for at in reversed(range(len(stages))):
-            if 0 <= step - at < count:
+            if stages[at] and 0 <= step - at < count:
                 stages[at](step - at)
                 if work:
                     work.pop(0)()

time: 134 us -> 96.8 us (0.72)
  Pallas kernels: 128 us -> 91.6 us
    pallas_call x1, Pallas kernels: 128 us -> 91.6 us  [correlate(): pl.pallas_call(correlate_kernel, out_shape=pltpu.VMEM((WIDE, 64, WIDE), j...]
where the time goes in v4:
time: 96.8 us; the launch traced here: 96.6 us
  Pallas kernels  91.6 us (95%)
  local copies, waits for them, and re-layouts  3.82 us (4%)
  other arithmetic  1.09 us (1%)
    pallas_call x1, Pallas kernels, correlate(): pl.pallas_call(correlate_kernel, out_shape=pltpu.VMEM((WIDE, 64, WIDE), j...  91.6 us
    unnamed x4, local copies, waits for them, and re-layouts  2.87 us

profile of v4, /device:TPU:16, one launch (start us, length us, event | category | flops | bytes accessed | tf_op | source)
XLA Modules:
  0.0 96.6 jit_solution(13115307507454704257)
XLA Ops:
  0.0 0.0 copy-start
  0.0 0.9 copy.7
  0.9 0.1 copy.8
  1.0 1.1 %broadcast_multiply_fusion = bf16[16,2,16,256]{3,2,1,0:T(8,128)(2,1)S(1)} fusion(bf16[16,2,16,256]{3,2,1,0:T(8,128)(2,1)} %param.3, bf16[16,16]{1,0:T(8,128)(2,1)S(1)} %copy.8), kind=kLoop, calls=%fused_computation.1 | loop fusion | flops 131072 | bytes 524800 | tf_op jit(solution)/shard_map/mul | solution.py:39
  2.0 0.2 reshape.7
  2.3 0.3 copy.9
  2.6 0.3 copy.10
  2.9 0.0 copy-done
  2.9 91.6 %correlate.1 = f32[128,64,128]{2,1,0:T(8,128)S(1)} custom-call(bf16[65,16,128]{2,1,0:T(8,128)(2,1)S(1)} %pad_maximum_fusion.unit, f32[4,128,512]{2,1,0:T(8,128)S(1)} %copy-done), custom_call_target="tpu_custom_call" | custom-call | tf_op jit(solution)/shard_map/correlate/pallas_call | solution.py:319
  94.6 2.0 %copy.12 = f32[128,64,128]{2,1,0:T(8,128)} copy(f32[128,64,128]{2,1,0:T(8,128)S(1)} %correlate.1) | data formatting | bytes 8388608
  (4 shorter events, 0.0 us)
Async XLA Ops:
  0.0 2.9 %copy-start = (f32[4,128,512]{2,1,0:T(8,128)S(1)}, f32[4,128,512]{2,1,0:T(8,128)}, u32[]{:S(2)}) copy-start(f32[4,128,512]{2,1,0:T(8,128)} %constant.5.clone.tables) | copy-start | bytes 3145732

commit v5 on v4

--- a/solution.py
+++ b/solution.py
@@ -15,10 +15,10 @@
 GROUPS = F // PACK
 SLOTS = GROUPS + 1
 WIDE = 128
-CHUNKS = "A5 B5 A6 B6 A6 B5 A5 B5 A5 B5 A5 B4 A3"
+CHUNKS = "B5 A5 M5 B5 A5 M4 B4 A5 M5 B5 A5 B5 A4 A3"
 KINDS = [name[0] for name in CHUNKS.split()]
 SIZES = [int(name[1:]) for name in CHUNKS.split()]
-IDLE = (1, 1, 2, 1, 0, 1)
+IDLE = (1, 1, 1, 1, 1, 0, 1, 1)
 ORDER = (0, 2, 1, 3)
 MESH = pl.DeviceIdType.MESH
 NT = (((1,), (1,)), ((), ()))
@@ -33,21 +33,17 @@
     return both.reshape(DAYS, LAGS // DAYS, 2 * F).astype(np.float32)
 
 
-def own_unit(spectra, validity):
+def pack_groups(spectra):
     windows, _, channels, _ = spectra.shape
-    flags = validity.astype(jnp.bfloat16)
-    cleaned = spectra * flags[:, None, :, None]
-    split = cleaned.reshape(windows, 2, channels, PACK, GROUPS)
-    packed = jnp.transpose(split, (4, 2, 3, 1, 0)).reshape(GROUPS, channels, WIDE)
-    first = jnp.pad(flags.T, ((0, 0), (0, WIDE - windows)))
-    return jnp.concatenate([first[None], packed])
+    split = spectra.reshape(windows, 2, channels, PACK, GROUPS)
+    return jnp.transpose(split, (4, 2, 3, 1, 0)).reshape(GROUPS, channels, WIDE)
 
 
 def swap8(block):
     return jnp.swapaxes(block, 0, 1)
 
 
-def correlate_kernel(unit, tables, out, near, full, stack, partial, exact, table, inverse, recv, sent, here, table_sem):
+def correlate_kernel(groups, validity, tables, out, near, full, stack, partial, exact, table, inverse, recv, sent, here, table_sem):
     row, col, day = lax.axis_index("row"), lax.axis_index("col"), lax.axis_index("day")
     core, x_hi, x_lo, y = row % 2, row // 2, col % 2, col // 2
     sibling = {"row": row + 1 - 2 * core}
@@ -76,6 +72,7 @@
     count = len(SIZES)
     spans = [pl.ds(sum(SIZES[:k]), SIZES[k]) for k in range(count)]
     mine, theirs = pl.ds(2 * core, 2), pl.ds(2 - 2 * core, 2)
+    my_unit = 2 * core + x_hi
     all_units, both, later = pl.ds(0, 4), pl.ds(0, 2), pl.ds(1, DAYS - 1)
     pending = [[] for _ in range(count)]
 
@@ -107,27 +104,50 @@
     def f_at(k, d, side, part=all_units):
         return full.at[d, spans[k], side, part]
 
-    def day_sends(k, block, place, slot, when=None):
-        for step in (1, 3, 2):
-            send(k, block, place(DAYS - step), slot + step - 1, days[step], when)
-
-    def day_arrivals(k, place, slot, when=None):
-        for step in (1, 3, 2):
-            arrive(k, place(DAYS - step), slot + step - 1, when)
+    def day_sends(k, place, slot, when=None):
+        send(k, place(0), place(DAYS - 1), slot, days[1], when)
+        send(k, place(0), place(1), slot + 2, days[DAYS - 1], when)
+
+    def day_forwards(k, place, half, slot, when=None):
+        arrive(k, place(DAYS - 1), slot, when)
+        send(k, half(DAYS - 1, 0), half(2, 0), slot + 1, days[1], when)
+        arrive(k, place(1), slot + 2, when)
+        send(k, half(1, 1), half(2, 1), 12 if slot == 2 else 13, days[DAYS - 1], when)
+
+    def day_arrivals(k, half, slot, when=None):
+        arrive(k, half(2, 0), slot + 1, when)
+        arrive(k, half(2, 1), 12 if slot == 2 else 13, when)
+
+    def near_blocks(k):
+        return lambda d: n_at(k, d, mine), lambda d, part: n_at(k, d, pl.ds(2 * core + part, 1))
+
+    def side_blocks(k):
+        return lambda d: f_at(k, d, x_lo), lambda d, part: f_at(k, d, x_lo, pl.ds(2 * part, 2))
+
+    def full_blocks(k):
+        return lambda d: f_at(k, d, both), lambda d, part: f_at(k, d, part)
+
+    def clean_unit():
+        windows, channels = validity.shape
+        lanes = lax.broadcasted_iota(jnp.int32, (windows, WIDE), 1) % windows
+        spread = (lanes == lax.broadcasted_iota(jnp.int32, (windows, WIDE), 0)).astype(jnp.bfloat16)
+        flags = validity[...].astype(jnp.float32).astype(jnp.bfloat16)
+        flags = lax.dot_general(flags, spread, (((0,), (0,)), ((), ())), preferred_element_type=jnp.float32)
+        first = lax.broadcasted_iota(jnp.int32, (channels, WIDE), 1) < windows
+        near[0, 0, my_unit] = jnp.where(first, flags, 0.0).astype(jnp.bfloat16)
+        flags = flags.astype(jnp.bfloat16)
+        for at in range(GROUPS):
+            near[0, at + 1, my_unit] = groups[at] * flags
 
     def start_units(k):
-        place = near.at[0, spans[k], 2 * core + x_hi]
-        send(k, unit.at[spans[k]], place, 0, opposite)
-        copy = pltpu.make_async_copy(unit.at[spans[k]], place, here.at[k, 0])
-        copy.start()
-        return copy
+        place = near.at[0, spans[k], my_unit]
+        send(k, place, place, 0, opposite)
 
     def spread_units(k):
         arrive(k, near.at[0, spans[k], 2 * core + 1 - x_hi], 0)
-        copies[k].wait()
         block = n_at(k, 0, mine)
         send(k, block, block, 1, sibling)
-        day_sends(k, block, lambda d: n_at(k, d, mine), 2, other_chip)
+        day_sends(k, near_blocks(k)[0], 2, other_chip)
 
     def first_spread(k):
         arrive(k, n_at(k, 0, theirs), 1)
@@ -141,7 +161,7 @@
 
         if KINDS[k] == "A":
             send(k, block, place, 6, up_y, home)
-            send(k, block, place, 6, down_y, home, extra=6)
+            send(k, block, place, 6, down_y, home, extra=8)
         else:
             send(k, block, place, 6, partner, home)
 
@@ -151,29 +171,36 @@
             arrive(k, block, 6, away)
             send(k, block, block, 6, up_y, relay_up)
             send(k, block, block, 6, down_y, relay_down)
-            day_sends(k, block, lambda d: f_at(k, d, x_lo), 7)
+            day_sends(k, side_blocks(k)[0], 7)
             send(k, block, block, 10, partner)
         else:
             arrive(k, f_at(k, 0, 1 - x_lo), 6, home)
             block = f_at(k, 0, both)
-            day_sends(k, block, lambda d: f_at(k, d, both), 7, home)
+            day_sends(k, full_blocks(k)[0], 7, home)
             send(k, block, block, 10, up_y, home)
-            send(k, block, block, 10, down_y, home, extra=3)
+            send(k, block, block, 10, down_y, home, extra=5)
+
+    def beside_days(k):
+        day_forwards(k, *near_blocks(k), 2, other_chip)
+        if KINDS[k] == "A":
+            day_forwards(k, *side_blocks(k), 7)
+        else:
+            day_forwards(k, *full_blocks(k), 7, home)
 
     def later_days(k):
-        day_arrivals(k, lambda d: n_at(k, d, mine), 2, other_chip)
+        day_arrivals(k, near_blocks(k)[1], 2, other_chip)
         block = n_at(k, later, mine)
         send(k, block, block, 5, sibling, other_chip)
         if KINDS[k] == "A":
-            day_arrivals(k, lambda d: f_at(k, d, x_lo), 7)
+            day_arrivals(k, side_blocks(k)[1], 7)
             block = f_at(k, later, x_lo)
             send(k, block, block, 11, partner)
         else:
-            day_arrivals(k, lambda d: f_at(k, d, both), 7, home)
+            day_arrivals(k, full_blocks(k)[1], 7, home)
             if KINDS[k] == "B":
                 block = f_at(k, later, both)
                 send(k, block, block, 11, up_y, home)
-                send(k, block, block, 11, down_y, home, extra=3)
+                send(k, block, block, 11, down_y, home, extra=5)
         block, place = f_at(k, later, x_lo), n_at(k, later)
         send(k, block, place, 5, sibling, home)
         act(home, lambda: pltpu.make_async_copy(block, place, here.at[k, 0]).start())
@@ -182,14 +209,18 @@
         if KINDS[k] != "A":
             relay(k, f_at(k, 0, both), 10)
         if KINDS[k] == "M":
-            day_sends(k, f_at(k, 0, both), lambda d: f_at(k, d, both), 7, beside)
+            day_sends(k, full_blocks(k)[0], 7, beside)
 
     def relay_later(k):
         if KINDS[k] == "B":
             relay(k, f_at(k, later, both), 11)
         if KINDS[k] == "M":
             arrive(k, f_at(k, 0, both), 10, far)
-            day_sends(k, f_at(k, 0, both), lambda d: f_at(k, d, both), 7, far)
+            day_sends(k, full_blocks(k)[0], 7, far)
+
+    def last_days(k):
+        if KINDS[k] == "M":
+            day_forwards(k, *full_blocks(k), 7, away)
 
     def relay(k, block, slot):
         arrive(k, block, slot, beside)
@@ -207,7 +238,7 @@
             arrive(k, f_at(k, 0, both), 10, far)
             arrive(k, f_at(k, later, both), 11, far)
         else:
-            day_arrivals(k, lambda d: f_at(k, d, both), 7, away)
+            day_arrivals(k, full_blocks(k)[1], 7, away)
 
     lane = lax.broadcasted_iota(jnp.int32, (64, 2 * WIDE), 1)
     real = (lane // 16) % 2 == 0
@@ -251,22 +282,25 @@
 
     def half_lags(j, half):
         span = pl.ds(half * F, F)
-        values = stack[j, span, :]
+        values = jnp.concatenate([stack[j, span, :], stack[j + 1, span, :]], axis=1)
         high = values.astype(jnp.bfloat16)
         low = (values - high.astype(jnp.float32)).astype(jnp.bfloat16)
         first = jnp.dot(table[:, span], high, preferred_element_type=jnp.float32)
         second = jnp.dot(table[:WIDE, span], low, preferred_element_type=jnp.float32)
-        return first[:WIDE] + first[WIDE:] + second
+        lags = first[:WIDE] + first[WIDE:] + second
+        return lags[:, :WIDE], lags[:, WIDE:]
 
     def first_half(group):
-        for at in range(8):
-            partial[group * 8 + at] = half_lags(group * 8 + at, 0)
+        for at in range(0, 8, 2):
+            j = group * 8 + at
+            partial[j], partial[j + 1] = half_lags(j, 0)
 
     def second_half(group):
         done = []
-        for at in range(8):
+        for at in range(0, 8, 2):
             j = group * 8 + at
-            done.append(((partial[j] + half_lags(j, 1)) * inverse[pl.ds(j, 1), :]).T)
+            for k, lags in enumerate(half_lags(j, 1)):
+                done.append(((partial[j + k] + lags) * inverse[pl.ds(j + k, 1), :]).T)
         start = pl.multiple_of(group * 8, 8)
         for at in range(0, WIDE, 8):
             out[at : at + 8, pl.ds(start, 8), :] = swap8(jnp.stack([d[at : at + 8] for d in done]))
@@ -290,13 +324,16 @@
             for at in range(0, 8, 2):
                 work.append(lambda first=at: repeat(first_half, first, 2))
 
+    clean_unit()
     pl.semaphore_wait(barrier, 8)
-    copies = [start_units(k) for k in range(count)]
+    for k in range(count):
+        start_units(k)
     stages = [spread_units]
-    for idle, stage in zip(IDLE, (first_spread, own_day, later_days, relay_own, relay_later, finish)):
+    order = (first_spread, own_day, beside_days, later_days, relay_own, relay_later, last_days, finish)
+    for idle, stage in zip(IDLE, order):
         stages += [None] * idle + [stage]
     for step in range(count + len(stages) - 1):
-        for at in reversed(range(len(stages))):
+        for at in range(len(stages)):
             if stages[at] and 0 <= step - at < count:
                 stages[at](step - at)
                 if work:
@@ -312,35 +349,35 @@
     sent_all(count - 1)
 
 
-def correlate(unit, tables):
+def correlate(groups, validity, tables):
     count = len(SIZES)
-    channels = unit.shape[1]
+    channels = groups.shape[1]
     vmem = pl.BlockSpec(memory_space=pltpu.VMEM)
     return pl.pallas_call(
         correlate_kernel,
         out_shape=pltpu.VMEM((WIDE, 64, WIDE), jnp.float32),
-        in_specs=[vmem, pl.BlockSpec(memory_space=pl.ANY)],
+        in_specs=[vmem, vmem, pl.BlockSpec(memory_space=pltpu.HBM)],
         out_specs=vmem,
         scratch_shapes=[
-            pltpu.VMEM((DAYS, SLOTS, 4, channels, WIDE), unit.dtype),
-            pltpu.VMEM((DAYS, SLOTS, 2, 4, channels, WIDE), unit.dtype),
+            pltpu.VMEM((DAYS, SLOTS, 4, channels, WIDE), groups.dtype),
+            pltpu.VMEM((DAYS, SLOTS, 2, 4, channels, WIDE), groups.dtype),
             pltpu.VMEM((64, 2 * F, WIDE), jnp.float32),
             pltpu.VMEM((64, WIDE, WIDE), jnp.float32),
             pltpu.VMEM((WIDE, 2 * F), jnp.float32),
             pltpu.VMEM((2 * WIDE, 2 * F), jnp.bfloat16),
             pltpu.VMEM((64, WIDE), jnp.float32),
-            pltpu.SemaphoreType.DMA((count, 12)),
-            pltpu.SemaphoreType.DMA((count, 15)),
+            pltpu.SemaphoreType.DMA((count, 14)),
+            pltpu.SemaphoreType.DMA((count, 17)),
             pltpu.SemaphoreType.DMA((count, 2)),
             pltpu.SemaphoreType.DMA,
         ],
         compiler_params=pltpu.CompilerParams(collective_id=0, has_side_effects=True, vmem_limit_bytes=44 << 20),
         name="correlate",
-    )(unit, tables)
+    )(groups, validity, tables)
 
 
 def per_device(spectra, validity):
-    return correlate(own_unit(spectra, validity), jnp.asarray(lag_tables()))
+    return correlate(pack_groups(spectra), validity, jnp.asarray(lag_tables()))
 
 
 def solution(mesh):

time: 96.8 us -> 93.3 us (0.964); the launches traced: 96.6 us -> 91.9 us
  Pallas kernels: 91.6 us -> 86.1 us
  local copies, waits for them, and re-layouts: 3.82 us -> 5.78 us
  other arithmetic: 1.09 us -> 0 us
    pallas_call x1, Pallas kernels: 91.6 us -> 86.1 us  [correlate(): pl.pallas_call(correlate_kernel, out_shape=pltpu.VMEM((WIDE, 64, WIDE), j...]
    unnamed x4 -> x5, local copies, waits for them, and re-layouts: 2.87 us -> 3.93 us
    mul x1 -> x0, other arithmetic: 1.05 us -> none  [own_unit(): cleaned = spectra * flags[:, None, :, None]]
    reshape x3, local copies, waits for them, and re-layouts: 0.86 us -> 1.85 us  [the longest x2 1.58 us: pack_groups(): split = spectra.reshape(windows, 2, channels, PACK, GROUPS)]
where the time goes in v5:
time: 93.3 us; the launch traced here: 91.9 us
  Pallas kernels  86.1 us (92%)
  local copies, waits for them, and re-layouts  5.78 us (6%)
    pallas_call x1, Pallas kernels, correlate(): pl.pallas_call(correlate_kernel, out_shape=pltpu.VMEM((WIDE, 64, WIDE), j...  86.1 us
    unnamed x5, local copies, waits for them, and re-layouts  3.93 us

profile of v5, /device:TPU:16, one launch (start us, length us, event | category | flops | bytes accessed | tf_op | source)
XLA Modules:
  0.0 91.9 jit_solution(16601029734078272603)
XLA Ops:
  0.0 1.2 %reshape.6 = bf16[16,2,16,4,64]{4,3,2,1,0:T(4,128)(2,1)S(1)} reshape(bf16[16,2,16,256]{3,2,1,0:T(8,128)(2,1)} %param.3) | data formatting | bytes 524288 | tf_op jit(solution)/shard_map/reshape | solution.py:38
  1.2 0.3 copy.5
  1.6 0.3 copy.6.groups
  1.9 0.0 copy-start
  1.9 1.2 %copy-done = f32[4,128,512]{2,1,0:T(8,128)S(1)} copy-done((f32[4,128,512]{2,1,0:T(8,128)S(1)}, f32[4,128,512]{2,1,0:T(8,128)}, u32[]{:S(2)}) %copy-start) | copy-done | bytes 1048600
  3.1 0.0 copy-start.1
  3.1 0.7 copy-done.1
  3.8 86.1 %correlate.1 = f32[128,64,128]{2,1,0:T(8,128)S(1)} custom-call(bf16[64,16,128]{2,1,0:T(8,128)(2,1)S(1)} %copy.6.groups, s32[16,16]{1,0:T(8,128)S(1)} %copy-done.1, f32[4,128,512]{2,1,0:T(8,128)S(1)} %copy-done), custom_call_target="tpu_custom_call" | custom-call | tf_op jit(solution)/shard_map/correlate/pallas_call | solution.py:356
  89.9 2.0 %copy.8 = f32[128,64,128]{2,1,0:T(8,128)} copy(f32[128,64,128]{2,1,0:T(8,128)S(1)} %correlate.1) | data formatting | bytes 8388608
Async XLA Ops:
  1.9 1.2 %copy-start = (f32[4,128,512]{2,1,0:T(8,128)S(1)}, f32[4,128,512]{2,1,0:T(8,128)}, u32[]{:S(2)}) copy-start(f32[4,128,512]{2,1,0:T(8,128)} %constant.2.clone.tables) | copy-start | bytes 3145732
  3.1 0.7 copy-start.1

commit v6 on v5

--- a/solution.py
+++ b/solution.py
@@ -43,7 +43,9 @@
     return jnp.swapaxes(block, 0, 1)
 
 
-def correlate_kernel(groups, validity, tables, out, near, full, stack, partial, exact, table, inverse, recv, sent, here, table_sem):
+def correlate_kernel(
+    groups, validity, tables, out, near, full, stack, partial, exact, table, inverse, usable, recv, sent, here, fetch
+):
     row, col, day = lax.axis_index("row"), lax.axis_index("col"), lax.axis_index("day")
     core, x_hi, x_lo, y = row % 2, row // 2, col % 2, col // 2
     sibling = {"row": row + 1 - 2 * core}
@@ -66,7 +68,9 @@
     for peer in (sibling, opposite, partner, up_y, down_y, *days[1:]):
         pl.semaphore_signal(barrier, inc=1, device_id=peer, device_id_type=MESH)
 
-    table_copy = pltpu.make_async_copy(tables.at[day], exact, table_sem)
+    flag_copy = pltpu.make_async_copy(validity, usable, fetch.at[0])
+    flag_copy.start()
+    table_copy = pltpu.make_async_copy(tables.at[day], exact, fetch.at[1])
     table_copy.start()
 
     count = len(SIZES)
@@ -128,10 +132,11 @@
         return lambda d: f_at(k, d, both), lambda d, part: f_at(k, d, part)
 
     def clean_unit():
-        windows, channels = validity.shape
+        windows, channels = usable.shape
+        flag_copy.wait()
         lanes = lax.broadcasted_iota(jnp.int32, (windows, WIDE), 1) % windows
         spread = (lanes == lax.broadcasted_iota(jnp.int32, (windows, WIDE), 0)).astype(jnp.bfloat16)
-        flags = validity[...].astype(jnp.float32).astype(jnp.bfloat16)
+        flags = usable[...].astype(jnp.float32).astype(jnp.bfloat16)
         flags = lax.dot_general(flags, spread, (((0,), (0,)), ((), ())), preferred_element_type=jnp.float32)
         first = lax.broadcasted_iota(jnp.int32, (channels, WIDE), 1) < windows
         near[0, 0, my_unit] = jnp.where(first, flags, 0.0).astype(jnp.bfloat16)
@@ -352,11 +357,11 @@
 def correlate(groups, validity, tables):
     count = len(SIZES)
     channels = groups.shape[1]
-    vmem = pl.BlockSpec(memory_space=pltpu.VMEM)
+    vmem, anywhere = pl.BlockSpec(memory_space=pltpu.VMEM), pl.BlockSpec(memory_space=pl.ANY)
     return pl.pallas_call(
         correlate_kernel,
         out_shape=pltpu.VMEM((WIDE, 64, WIDE), jnp.float32),
-        in_specs=[vmem, vmem, pl.BlockSpec(memory_space=pltpu.HBM)],
+        in_specs=[vmem, anywhere, anywhere],
         out_specs=vmem,
         scratch_shapes=[
             pltpu.VMEM((DAYS, SLOTS, 4, channels, WIDE), groups.dtype),
@@ -366,18 +371,19 @@
             pltpu.VMEM((WIDE, 2 * F), jnp.float32),
             pltpu.VMEM((2 * WIDE, 2 * F), jnp.bfloat16),
             pltpu.VMEM((64, WIDE), jnp.float32),
+            pltpu.VMEM(validity.shape, validity.dtype),
             pltpu.SemaphoreType.DMA((count, 14)),
             pltpu.SemaphoreType.DMA((count, 17)),
             pltpu.SemaphoreType.DMA((count, 2)),
-            pltpu.SemaphoreType.DMA,
+            pltpu.SemaphoreType.DMA((2,)),
         ],
-        compiler_params=pltpu.CompilerParams(collective_id=0, has_side_effects=True, vmem_limit_bytes=44 << 20),
+        compiler_params=pltpu.CompilerParams(collective_id=0, has_side_effects=True, vmem_limit_bytes=58 << 20),
         name="correlate",
     )(groups, validity, tables)
 
 
 def per_device(spectra, validity):
-    return correlate(pack_groups(spectra), validity, jnp.asarray(lag_tables()))
+    return correlate(pltpu.with_memory_space_constraint(pack_groups(spectra), pltpu.VMEM), validity, jnp.asarray(lag_tables()))
 
 
 def solution(mesh):

time: 93.3 us -> 91.5 us (0.981)
  local copies, waits for them, and re-layouts: 5.78 us -> 3.87 us
    unnamed x5 -> x1, local copies, waits for them, and re-layouts: 3.93 us -> 2.02 us
where the time goes in v6:
time: 91.5 us; the launch traced here: 90.2 us
  Pallas kernels  86.3 us (94%)
  local copies, waits for them, and re-layouts  3.87 us (4%)
    pallas_call x1, Pallas kernels, correlate(): pl.pallas_call(correlate_kernel, out_shape=pltpu.VMEM((WIDE, 64, WIDE), j...  86.3 us
    unnamed x1, local copies, waits for them, and re-layouts  2.02 us

profile of v6, /device:TPU:16, one launch (start us, length us, event | category | flops | bytes accessed | tf_op | source)
XLA Modules:
  0.0 90.2 jit_solution(17935919507391580304)
XLA Ops:
  0.0 1.2 %reshape.6 = bf16[16,2,16,4,64]{4,3,2,1,0:T(4,128)(2,1)S(1)} reshape(bf16[16,2,16,256]{3,2,1,0:T(8,128)(2,1)} %param.3) | data formatting | bytes 524288 | tf_op jit(solution)/shard_map/reshape | solution.py:38
  1.2 0.3 copy.5
  1.6 0.3 copy.6.groups
  1.9 86.3 %correlate.1 = f32[128,64,128]{2,1,0:T(8,128)S(1)} custom-call(bf16[64,16,128]{2,1,0:T(8,128)(2,1)S(1)} %copy.6.groups, s32[16,16]{1,0:T(8,128)} %validity.1, f32[4,128,512]{2,1,0:T(8,128)} %constant.2.clone.tables), custom_call_target="tpu_custom_call" | custom-call | tf_op jit(solution)/shard_map/correlate/pallas_call | solution.py:361
  88.2 2.0 %copy.8 = f32[128,64,128]{2,1,0:T(8,128)} copy(f32[128,64,128]{2,1,0:T(8,128)S(1)} %correlate.1) | data formatting | bytes 8388608

commit v7 on v6

--- a/solution.py
+++ b/solution.py
@@ -15,7 +15,7 @@
 GROUPS = F // PACK
 SLOTS = GROUPS + 1
 WIDE = 128
-CHUNKS = "B5 A5 M5 B5 A5 M4 B4 A5 M5 B5 A5 B5 A4 A3"
+CHUNKS = "B4 A4 M4 B4 A4 M4 B4 A5 B4 A4 M4 B4 A4 B4 A4 A4"
 KINDS = [name[0] for name in CHUNKS.split()]
 SIZES = [int(name[1:]) for name in CHUNKS.split()]
 IDLE = (1, 1, 1, 1, 1, 0, 1, 1)
@@ -35,8 +35,8 @@
 
 def pack_groups(spectra):
     windows, _, channels, _ = spectra.shape
-    split = spectra.reshape(windows, 2, channels, PACK, GROUPS)
-    return jnp.transpose(split, (4, 2, 3, 1, 0)).reshape(GROUPS, channels, WIDE)
+    split = jnp.transpose(spectra, (3, 2, 1, 0)).reshape(PACK, GROUPS, channels, 2 * windows)
+    return jnp.transpose(split, (1, 2, 0, 3)).reshape(GROUPS, channels, WIDE)
 
 
 def swap8(block):
@@ -44,7 +44,7 @@
 
 
 def correlate_kernel(
-    groups, validity, tables, out, near, full, stack, partial, exact, table, inverse, usable, recv, sent, here, fetch
+    groups, validity, tables, lags, near, full, stack, exact, table, inverse, usable, recv, sent, here, fetch
 ):
     row, col, day = lax.axis_index("row"), lax.axis_index("col"), lax.axis_index("day")
     core, x_hi, x_lo, y = row % 2, row // 2, col % 2, col // 2
@@ -292,23 +292,19 @@
         low = (values - high.astype(jnp.float32)).astype(jnp.bfloat16)
         first = jnp.dot(table[:, span], high, preferred_element_type=jnp.float32)
         second = jnp.dot(table[:WIDE, span], low, preferred_element_type=jnp.float32)
-        lags = first[:WIDE] + first[WIDE:] + second
-        return lags[:, :WIDE], lags[:, WIDE:]
+        total = first[:WIDE] + first[WIDE:] + second
+        return total[:, :WIDE], total[:, WIDE:]
 
     def first_half(group):
         for at in range(0, 8, 2):
             j = group * 8 + at
-            partial[j], partial[j + 1] = half_lags(j, 0)
+            lags[j], lags[j + 1] = half_lags(j, 0)
 
     def second_half(group):
-        done = []
         for at in range(0, 8, 2):
             j = group * 8 + at
-            for k, lags in enumerate(half_lags(j, 1)):
-                done.append(((partial[j + k] + lags) * inverse[pl.ds(j + k, 1), :]).T)
-        start = pl.multiple_of(group * 8, 8)
-        for at in range(0, WIDE, 8):
-            out[at : at + 8, pl.ds(start, 8), :] = swap8(jnp.stack([d[at : at + 8] for d in done]))
+            for k, half in enumerate(half_lags(j, 1)):
+                lags[j + k] = (lags[j + k] + half) * inverse[pl.ds(j + k, 1), :]
 
     def repeat(body, first, times):
         def step(at, _):
@@ -360,14 +356,13 @@
     vmem, anywhere = pl.BlockSpec(memory_space=pltpu.VMEM), pl.BlockSpec(memory_space=pl.ANY)
     return pl.pallas_call(
         correlate_kernel,
-        out_shape=pltpu.VMEM((WIDE, 64, WIDE), jnp.float32),
+        out_shape=pltpu.VMEM((64, WIDE, WIDE), jnp.float32),
         in_specs=[vmem, anywhere, anywhere],
         out_specs=vmem,
         scratch_shapes=[
             pltpu.VMEM((DAYS, SLOTS, 4, channels, WIDE), groups.dtype),
             pltpu.VMEM((DAYS, SLOTS, 2, 4, channels, WIDE), groups.dtype),
             pltpu.VMEM((64, 2 * F, WIDE), jnp.float32),
-            pltpu.VMEM((64, WIDE, WIDE), jnp.float32),
             pltpu.VMEM((WIDE, 2 * F), jnp.float32),
             pltpu.VMEM((2 * WIDE, 2 * F), jnp.bfloat16),
             pltpu.VMEM((64, WIDE), jnp.float32),
@@ -382,8 +377,28 @@
     )(groups, validity, tables)
 
 
+def arrange_kernel(lags, out):
+    group = pl.program_id(0)
+    turned = [lags[group * 8 + at].T for at in range(8)]
+    for at in range(0, WIDE, 8):
+        out[at : at + 8] = swap8(jnp.stack([tile[at : at + 8] for tile in turned]))
+
+
+def arrange(lags):
+    return pl.pallas_call(
+        arrange_kernel,
+        grid=(8,),
+        out_shape=jax.ShapeDtypeStruct((WIDE, 64, WIDE), jnp.float32),
+        in_specs=[pl.BlockSpec(memory_space=pltpu.VMEM)],
+        out_specs=pl.BlockSpec((WIDE, 8, WIDE), lambda group: (0, group, 0)),
+        compiler_params=pltpu.CompilerParams(vmem_limit_bytes=16 << 20),
+        name="arrange",
+    )(pltpu.with_memory_space_constraint(lags, pltpu.VMEM))
+
+
 def per_device(spectra, validity):
-    return correlate(pltpu.with_memory_space_constraint(pack_groups(spectra), pltpu.VMEM), validity, jnp.asarray(lag_tables()))
+    lags = correlate(pltpu.with_memory_space_constraint(pack_groups(spectra), pltpu.VMEM), validity, jnp.asarray(lag_tables()))
+    return arrange(lags)
 
 
 def solution(mesh):

time: 91.5 us -> 89.8 us (0.981)
  local copies, waits for them, and re-layouts: 3.87 us -> 1.73 us
  Pallas kernels: 86.3 us -> 87.4 us
    unnamed x1 -> x0, local copies, waits for them, and re-layouts: 2.02 us -> none
    reshape x3 -> x2, local copies, waits for them, and re-layouts: 1.85 us -> 0.52 us  [the longest x1 0.28 us: pack_groups(): return jnp.transpose(split, (1, 2, 0, 3)).reshape(GROUPS, channels, WIDE)]
    transpose x0 -> x2, local copies, waits for them, and re-layouts: none -> 1.21 us  [the longest x1 1.1 us: pack_groups(): jnp.transpose(spectra, (3, 2, 1, 0))]
    pallas_call x1 -> x2, Pallas kernels: 86.3 us -> 87.4 us  [the longest x1 83 us: correlate(): pl.pallas_call(correlate_kernel, out_shape=pltpu.VMEM((64, WIDE, WIDE), j...]
where the time goes in v7:
time: 89.8 us; the launch traced here: 89.1 us
  Pallas kernels  87.4 us (97%)
  local copies, waits for them, and re-layouts  1.73 us (2%)
    pallas_call x1, Pallas kernels, correlate(): pl.pallas_call(correlate_kernel, out_shape=pltpu.VMEM((64, WIDE, WIDE), j...  83 us
    pallas_call x1, Pallas kernels, arrange(): pl.pallas_call(arrange_kernel, grid=(8,), out_shape=jax.ShapeDtypeStruct(...  4.42 us

profile of v7, /device:TPU:16, one launch (start us, length us, event | category | flops | bytes accessed | tf_op | source)
XLA Modules:
  0.0 89.1 jit_solution(8351925942176660467)
XLA Ops:
  0.0 1.1 %copy.4 = bf16[256,16,2,16]{0,3,2,1:T(8,128)(2,1)S(1)} copy(bf16[256,16,2,16]{0,1,2,3:T(8,128)(2,1)} %bitcast.9) | data formatting | bytes 524288 | tf_op jit(solution)/shard_map/transpose | solution.py:38
  1.1 0.2 reshape.6
  1.3 0.1 copy.5
  1.5 0.3 copy.6.groups
  1.8 83.0 %correlate.1.lags = f32[64,128,128]{2,1,0:T(8,128)S(1)} custom-call(bf16[64,16,128]{2,1,0:T(8,128)(2,1)S(1)} %copy.6.groups, s32[16,16]{1,0:T(8,128)} %validity.1, f32[4,128,512]{2,1,0:T(8,128)} %constant.2.clone.tables), custom_call_target="tpu_custom_call" | custom-call | tf_op jit(solution)/shard_map/correlate/pallas_call | solution.py:357
  84.7 4.4 %arrange.1 = f32[128,64,128]{2,1,0:T(8,128)} custom-call(f32[64,128,128]{2,1,0:T(8,128)S(1)} %correlate.1.lags), custom_call_target="tpu_custom_call" | custom-call | tf_op jit(solution)/shard_map/arrange/pallas_call | solution.py:388

commit v8 on v7

--- a/solution.py
+++ b/solution.py
@@ -378,19 +378,21 @@
 
 
 def arrange_kernel(lags, out):
-    group = pl.program_id(0)
-    turned = [lags[group * 8 + at].T for at in range(8)]
-    for at in range(0, WIDE, 8):
-        out[at : at + 8] = swap8(jnp.stack([tile[at : at + 8] for tile in turned]))
+    width = out.shape[1]
+    for first in range(0, width, 8):
+        start = pl.program_id(0) * width + first
+        turned = [lags[start + at].T for at in range(8)]
+        for at in range(0, WIDE, 8):
+            out[at : at + 8, first : first + 8] = swap8(jnp.stack([tile[at : at + 8] for tile in turned]))
 
 
 def arrange(lags):
     return pl.pallas_call(
         arrange_kernel,
-        grid=(8,),
+        grid=(2,),
         out_shape=jax.ShapeDtypeStruct((WIDE, 64, WIDE), jnp.float32),
         in_specs=[pl.BlockSpec(memory_space=pltpu.VMEM)],
-        out_specs=pl.BlockSpec((WIDE, 8, WIDE), lambda group: (0, group, 0)),
+        out_specs=pl.BlockSpec((WIDE, 32, WIDE), lambda half: (0, half, 0)),
         compiler_params=pltpu.CompilerParams(vmem_limit_bytes=16 << 20),
         name="arrange",
     )(pltpu.with_memory_space_constraint(lags, pltpu.VMEM))

time: 89.8 us -> 88.3 us (0.983)
  Pallas kernels: 87.4 us -> 85.9 us
    pallas_call x1, Pallas kernels: 4.42 us -> 2.92 us  [arrange(): pl.pallas_call(arrange_kernel, grid=(2,), out_shape=jax.ShapeDtypeStruct(...]
where the time goes in v8:
time: 88.3 us; the launch traced here: 87.6 us
  Pallas kernels  85.9 us (97%)
  local copies, waits for them, and re-layouts  1.73 us (2%)
    pallas_call x1, Pallas kernels, correlate(): pl.pallas_call(correlate_kernel, out_shape=pltpu.VMEM((64, WIDE, WIDE), j...  83 us
    pallas_call x1, Pallas kernels, arrange(): pl.pallas_call(arrange_kernel, grid=(2,), out_shape=jax.ShapeDtypeStruct(...  2.92 us

profile of v8, /device:TPU:16, one launch (start us, length us, event | category | flops | bytes accessed | tf_op | source)
XLA Modules:
  0.0 87.6 jit_solution(9224283222546772983)
XLA Ops:
  0.0 1.1 %copy.4 = bf16[256,16,2,16]{0,3,2,1:T(8,128)(2,1)S(1)} copy(bf16[256,16,2,16]{0,1,2,3:T(8,128)(2,1)} %bitcast.9) | data formatting | bytes 524288 | tf_op jit(solution)/shard_map/transpose | solution.py:38
  1.1 0.2 reshape.6
  1.3 0.1 copy.5
  1.5 0.3 copy.6.groups
  1.8 83.0 %correlate.1.lags = f32[64,128,128]{2,1,0:T(8,128)S(1)} custom-call(bf16[64,16,128]{2,1,0:T(8,128)(2,1)S(1)} %copy.6.groups, s32[16,16]{1,0:T(8,128)} %validity.1, f32[4,128,512]{2,1,0:T(8,128)} %constant.2.clone.tables), custom_call_target="tpu_custom_call" | custom-call | tf_op jit(solution)/shard_map/correlate/pallas_call | solution.py:357
  84.7 2.9 %arrange.1 = f32[128,64,128]{2,1,0:T(8,128)} custom-call(f32[64,128,128]{2,1,0:T(8,128)S(1)} %correlate.1.lags), custom_call_target="tpu_custom_call" | custom-call | tf_op jit(solution)/shard_map/arrange/pallas_call | solution.py:390
